TPU v7x, 128 devices: a whole 4x4x4 slice. The times are simulated.
128 devices in a mesh: dp: 8 (over x, core), tensor: 16 (over z, y).
Axes of the slice: x: 4, y: 4, z: 4, core: 2. Of those that a mesh axis runs over, the one named last changes fastest.
Arguments:
- gate_grad: float32 [8, 256, 28672], P('dp', 'tensor'), may hold values from -6 to 6
- up_grad: float32 [8, 256, 28672], P('dp', 'tensor'), may hold values from -6 to 6
- down_grad: float32 [8, 256, 8192], P('dp', 'tensor'), may hold values from -6 to 6
- gate_error: bfloat16 [8, 256, 28672], P('dp', 'tensor'), may hold values from -4 to 4
- up_error: bfloat16 [8, 256, 28672], P('dp', 'tensor'), may hold values from -4 to 4
- down_error: bfloat16 [8, 256, 8192], P('dp', 'tensor'), may hold values from -4 to 4
- gate_right: float32 [4, 28672], replicated, may hold values from -0.03125 to 0.03125
- up_right: float32 [4, 28672], replicated, may hold values from -0.03125 to 0.03125
- down_right: float32 [4, 8192], replicated, may hold values from -0.0625 to 0.0625
Outputs:
- gate_left: float32 [4, 256], P(None, 'tensor')
- up_left: float32 [4, 256], P(None, 'tensor')
- down_left: float32 [4, 256], P(None, 'tensor')
- gate_right_next: float32 [4, 28672], replicated
- up_right_next: float32 [4, 28672], replicated
- down_right_next: float32 [4, 8192], replicated
- gate_error_next: bfloat16 [8, 256, 28672], P('dp', 'tensor')
- up_error_next: bfloat16 [8, 256, 28672], P('dp', 'tensor')
- down_error_next: bfloat16 [8, 256, 8192], P('dp', 'tensor')
All inputs are finite; a program needn't handle non-finite values.
Results may differ from a plain program's by a relative error of at most 0.001.
Values sent between devices are 32-bit elements; how exact they have to be, the bound alone decides.
No kernel may reach another device: no remote copies, remote signals or barrier semaphores. Data moves between devices by JAX's collectives and lax.ppermute only.
A program may use at most 128 MiB of HBM per device.

v0:
```python
import jax
import jax.numpy as jnp
from jax import lax
from jax.sharding import PartitionSpec as P


def contract_columns(right, merged):
    return lax.dot_general(right, merged, (((1,), (1,)), ((), ())), precision=lax.Precision.HIGHEST)


def contract_rows(left, merged):
    return lax.dot_general(left, merged, (((1,), (0,)), ((), ())), precision=lax.Precision.HIGHEST)


def per_device(
    gate_grad,
    up_grad,
    down_grad,
    gate_error,
    up_error,
    down_error,
    gate_right,
    up_right,
    down_right,
):
    highest = lax.Precision.HIGHEST
    replicas = lax.axis_size("dp")
    merged = [
        gate_grad[0] + gate_error[0].astype(jnp.float32),
        up_grad[0] + up_error[0].astype(jnp.float32),
        down_grad[0] + down_error[0].astype(jnp.float32),
    ]
    rights = [gate_right, up_right, down_right]
    partial_value = [contract_columns(rights[m_index], merged[m_index]) for m_index in range(3)]
    summed = lax.psum((partial_value[0], partial_value[1], partial_value[2]), "dp")
    lefts = [piece / replicas for piece in summed]
    rank = lefts[0].shape[0]
    built = [[], [], []]
    for row_index in range(rank):
        current = [left[row_index] for left in lefts]
        if row_index > 0:
            earlier = [jnp.stack(rows) for rows in built]
            inner = [
                jnp.dot(earlier[m_index], current[m_index], precision=highest)
                for m_index in range(3)
            ]
            inner = lax.psum((inner[0], inner[1], inner[2]), "tensor")
            current = [
                current[m_index] - jnp.dot(inner[m_index], earlier[m_index], precision=highest)
                for m_index in range(3)
            ]
        squares = [jnp.sum(item * item) for item in current]
        lengths = lax.psum((squares[0], squares[1], squares[2]), "tensor")
        for m_index in range(3):
            built[m_index].append(current[m_index] / jnp.sqrt(lengths[m_index]))
    bases = [jnp.stack(rows) for rows in built]
    terms = [contract_rows(bases[m_index], merged[m_index]) for m_index in range(3)]
    across = lax.psum((terms[0], terms[1], terms[2]), "tensor")
    totals = lax.psum((across[0], across[1], across[2]), "dp")
    nexts = [total / replicas for total in totals]
    errors = []
    for m_index in range(3):
        approx = lax.dot_general(
            bases[m_index], nexts[m_index], (((0,), (0,)), ((), ())), precision=highest
        )
        errors.append((merged[m_index] - approx).astype(jnp.bfloat16)[None])
    return (
        bases[0],
        bases[1],
        bases[2],
        nexts[0],
        nexts[1],
        nexts[2],
        errors[0],
        errors[1],
        errors[2],
    )


def solution(mesh):
    in_specs = (
        P("dp", "tensor", None),
        P("dp", "tensor", None),
        P("dp", "tensor", None),
        P("dp", "tensor", None),
        P("dp", "tensor", None),
        P("dp", "tensor", None),
        P(),
        P(),
        P(),
    )
    out_specs = (
        P(None, "tensor"),
        P(None, "tensor"),
        P(None, "tensor"),
        P(),
        P(),
        P(),
        P("dp", "tensor", None),
        P("dp", "tensor", None),
        P("dp", "tensor", None),
    )
    return jax.shard_map(
        per_device, mesh=mesh, in_specs=in_specs, out_specs=out_specs, check_vma=False
    )
```

profile of v0, /device:TPU:1, one launch (start us, length us, event | category | flops | bytes accessed | tf_op | source)
XLA Modules:
  0.0 486.4 jit_solution(12244305040144040601)
XLA Ops:
  7.3 0.9 copy-done
  8.2 4.1 fusion.14
  12.3 2.3 fusion.17
  15.4 13.4 %all-reduce.8 = (f32[4,16]{1,0:T(4,128)S(1)}, f32[4,16]{1,0:T(4,128)S(1)}, f32[4,16]{1,0:T(4,128)S(1)}) all-reduce(f32[4,16]{1,0:T(4,128)S(1)} %fusion.14, f32[4,16]{1,0:T(4,128)S(1)} %fusion.17, f32[4,16]{1,0:T(4,128)S(1)} %convolution_bitcast_fusion), channel_id=1, replica_groups=mesh['dp'=8,'tensor'=16] {'dp'}, use_global_device_ids=true, to_apply=%region_0.0 | all-reduce | flops 192 | bytes 1536 | tf_op jit(solution)/shard_map/psum | solution.py:35
  30.6 35.8 %all-reduce.6 = (f32[]{:T(128)}, f32[]{:T(128)}, f32[]{:T(128)}) all-reduce(f32[]{:T(128)} %multiply_reduce_fusion.11, f32[]{:T(128)} %multiply_reduce_fusion.7, f32[]{:T(128)} %multiply_reduce_fusion.3), channel_id=1, replica_groups=mesh['dp'=8,'tensor'=16] {'tensor'}, use_global_device_ids=true, to_apply=%region_2.0 | all-reduce | flops 3 | bytes 24 | tf_op jit(solution)/shard_map/psum | solution.py:53
  70.3 29.2 %all-reduce.5 = (f32[]{:T(128)}, f32[]{:T(128)}, f32[]{:T(128)}) all-reduce(f32[]{:T(128)} %get-tuple-element.43, f32[]{:T(128)} %get-tuple-element.41, f32[]{:T(128)} %get-tuple-element.39), channel_id=1, replica_groups=mesh['dp'=8,'tensor'=16] {'tensor'}, use_global_device_ids=true, to_apply=%region_3.0 | all-reduce | flops 3 | bytes 24 | tf_op jit(solution)/shard_map/psum | solution.py:47
  99.5 1.2 multiply_reduce_fusion.2
  100.7 1.2 multiply_reduce_fusion.6
  102.0 1.2 multiply_reduce_fusion.10
  103.2 30.8 %all-reduce.4 = (f32[]{:T(128)}, f32[]{:T(128)}, f32[]{:T(128)}) all-reduce(f32[]{:T(128)} %multiply_reduce_fusion.10, f32[]{:T(128)} %multiply_reduce_fusion.6, f32[]{:T(128)} %multiply_reduce_fusion.2), channel_id=1, replica_groups=mesh['dp'=8,'tensor'=16] {'tensor'}, use_global_device_ids=true, to_apply=%region_5.0 | all-reduce | flops 3 | bytes 24 | tf_op jit(solution)/shard_map/psum | solution.py:53
  138.5 28.5 %all-reduce.3 = (f32[2]{0:T(128)S(1)}, f32[2]{0:T(128)S(1)}, f32[2]{0:T(128)S(1)}) all-reduce(f32[2]{0:T(128)S(1)} %convolution_bitcast_fusion.12, f32[2]{0:T(128)S(1)} %convolution_bitcast_fusion.10, f32[2]{0:T(128)S(1)} %convolution_bitcast_fusion.8), channel_id=1, replica_groups=mesh['dp'=8,'tensor'=16] {'tensor'}, use_global_device_ids=true, to_apply=%region_6.0 | all-reduce | flops 6 | bytes 48 | tf_op jit(solution)/shard_map/psum | solution.py:47
  169.2 31.3 %all-reduce.2 = (f32[]{:T(128)}, f32[]{:T(128)}, f32[]{:T(128)}) all-reduce(f32[]{:T(128)} %get-tuple-element.45, f32[]{:T(128)} %get-tuple-element.47, f32[]{:T(128)} %get-tuple-element.49), channel_id=1, replica_groups=mesh['dp'=8,'tensor'=16] {'tensor'}, use_global_device_ids=true, to_apply=%region_8.0 | all-reduce | flops 3 | bytes 24 | tf_op jit(solution)/shard_map/psum | solution.py:53
  203.1 28.5 %all-reduce.1 = (f32[3]{0:T(128)S(1)}, f32[3]{0:T(128)S(1)}, f32[3]{0:T(128)S(1)}) all-reduce(f32[3]{0:T(128)S(1)} %convolution_bitcast_fusion.6, f32[3]{0:T(128)S(1)} %convolution_bitcast_fusion.4, f32[3]{0:T(128)S(1)} %convolution_bitcast_fusion.2), channel_id=1, replica_groups=mesh['dp'=8,'tensor'=16] {'tensor'}, use_global_device_ids=true, to_apply=%region_9.0 | all-reduce | flops 9 | bytes 72 | tf_op jit(solution)/shard_map/psum | solution.py:47
  233.8 30.6 %all-reduce = (f32[]{:T(128)}, f32[]{:T(128)}, f32[]{:T(128)}) all-reduce(f32[]{:T(128)} %get-tuple-element.51, f32[]{:T(128)} %get-tuple-element.53, f32[]{:T(128)} %get-tuple-element.55), channel_id=1, replica_groups=mesh['dp'=8,'tensor'=16] {'tensor'}, use_global_device_ids=true, to_apply=%region_11.0 | all-reduce | flops 3 | bytes 24 | tf_op jit(solution)/shard_map/psum | solution.py:53
  266.6 2.1 fusion.26
  268.7 3.6 fusion.10
  272.3 1.8 fusion.6
  274.4 130.8 %all-reduce.13.cloned.1.call-done = (f32[4,28672]{1,0:T(4,128)}, f32[4,28672]{1,0:T(4,128)}, f32[4,8192]{1,0:T(4,128)}) async-done(((f32[4,28672]{1,0:T(4,128)}, f32[4,28672]{1,0:T(4,128)}, f32[4,8192]{1,0:T(4,128)}), (f32[4,28672]{1,0:T(4,128)}, f32[4,28672]{1,0:T(4,128)}, f32[4,8192]{1,0:T(4,128)})) %all-reduce.13.cloned.1.call-update) | async-done | bytes 1048592 | tf_op jit(solution)/shard_map/psum | solution.py:58
  405.2 64.1 %all-reduce.15.cloned.1.call-done = (f32[4,28672]{1,0:T(4,128)}, f32[4,28672]{1,0:T(4,128)}, f32[4,8192]{1,0:T(4,128)}) async-done(((f32[4,28672]{1,0:T(4,128)}, f32[4,28672]{1,0:T(4,128)}, f32[4,8192]{1,0:T(4,128)}), (f32[4,28672]{1,0:T(4,128)}, f32[4,28672]{1,0:T(4,128)}, f32[4,8192]{1,0:T(4,128)})) %all-reduce.15.cloned.1.call-update) | async-done | bytes 1048592 | tf_op jit(solution)/shard_map/psum | solution.py:59
  469.3 1.2 broadcast_multiply_fusion.1
  470.5 1.1 broadcast_multiply_fusion.2
  471.6 2.5 fusion.5
  474.2 2.7 fusion.2
  476.9 2.7 fusion.3
  (69 shorter events, 12.1 us)
Async XLA Ops:
  7.2 1.0 copy-start
  7.2 5.1 %copy-start.3 = (bf16[1,16,28672]{2,1,0:T(8,128)(2,1)S(1)}, bf16[1,16,28672]{2,1,0:T(8,128)(2,1)}, u32[]{:S(2)}) copy-start(bf16[1,16,28672]{2,1,0:T(8,128)(2,1)} %param.13) | copy-start | bytes 2752516
  7.2 5.1 %copy-start.1 = (f32[1,16,28672]{2,1,0:T(8,128)S(1)}, f32[1,16,28672]{2,1,0:T(8,128)}, u32[]{:S(2)}) copy-start(f32[1,16,28672]{2,1,0:T(8,128)} %param.10) | copy-start | bytes 5505028
  7.2 398.0 %all-reduce.13.cloned.1.call-start = ((), (), s32[]{:S(2)}) async-start(), calls=%async_computation | async-start | bytes 2097152 | tf_op jit(solution)/shard_map/psum | solution.py:58
  8.2 4.1 copy-start.11
  12.3 2.4 copy-start.5
  12.3 2.4 copy-start.6
  12.3 2.4 copy-start.12
  266.5 205.0 %copy-start.15 = (f32[4,16]{1,0:T(4,128)}, f32[4,16]{1,0:T(4,128)S(1)}, u32[]{:S(2)}) copy-start(f32[4,16]{1,0:T(4,128)S(1)} %pad_maximum_fusion.5) | copy-start | bytes 772
  266.6 207.6 %copy-start.13 = (f32[4,16]{1,0:T(4,128)}, f32[4,16]{1,0:T(4,128)S(1)}, u32[]{:S(2)}) copy-start(f32[4,16]{1,0:T(4,128)S(1)} %pad_maximum_fusion.3) | copy-start | bytes 772
  266.6 210.3 %copy-start.14 = (f32[4,16]{1,0:T(4,128)}, f32[4,16]{1,0:T(4,128)S(1)}, u32[]{:S(2)}) copy-start(f32[4,16]{1,0:T(4,128)S(1)} %pad_maximum_fusion.1) | copy-start | bytes 772
  274.2 195.1 %all-reduce.15.cloned.1.call-start = ((), (), s32[]{:S(2)}) async-start(), calls=%async_computation.1 | async-start | bytes 2097152 | tf_op jit(solution)/shard_map/psum | solution.py:59
  469.3 4.7 copy-start.10
  470.5 6.4 %copy-start.7 = (f32[4,28672]{1,0:T(4,128)}, f32[4,28672]{1,0:T(4,128)S(1)}, u32[]{:S(2)}) copy-start(f32[4,28672]{1,0:T(4,128)S(1)} %broadcast_multiply_fusion.1) | copy-start | bytes 1376260
  471.6 5.3 %copy-start.9 = (f32[4,8192]{1,0:T(4,128)}, f32[4,8192]{1,0:T(4,128)S(1)}, u32[]{:S(2)}) copy-start(f32[4,8192]{1,0:T(4,128)S(1)} %broadcast_multiply_fusion.2) | copy-start | bytes 393220
  474.2 2.7 copy-start.8
  474.2 2.7 copy-start.2
  474.2 2.7 copy-start.4
Sparse Core Ops, SparseCore 0:
  274.3 130.8 all-reduce.12
  407.7 61.5 all-reduce.14
where the time goes:
time: 488 us; the launch traced here: 486 us
  blocking collectives  228 us (47%)
  waiting for transfers between devices  195 us (40%)
  matrix products  27.7 us (6%)
  between operations  22.6 us (5%)
  other arithmetic  11.7 us (2%)
    psum x1, waiting for transfers between devices, per_device(): across = lax.psum((terms[0], terms[1], terms[2]), 'tensor')  131 us
    psum x4, blocking collectives, per_device(): lengths = lax.psum((squares[0], squares[1], squares[2]), 'tensor')  129 us
    psum x3, blocking collectives, per_device(): inner = lax.psum((inner[0], inner[1], inner[2]), 'tensor')  86.2 us
    psum x1, waiting for transfers between devices, per_device(): totals = lax.psum((across[0], across[1], across[2]), 'dp')  64.1 us
    psum x1, blocking collectives, per_device(): lax.psum((partial_value[0], partial_value[1], partial_value[2]), 'dp')  13.4 us
  transfers between devices with their start and end apart: 2, of which 2 were waited for; matrix products, arithmetic and copies ran while one was open for 0% of the time, Pallas kernels for 0%

commit v1 on v0

v1 whole, which is shorter than its diff:
```python
import functools

import jax
import jax.numpy as jnp
from jax import lax
from jax.experimental import pallas as pl
from jax.experimental.pallas import tpu as pltpu
from jax.sharding import PartitionSpec as P

F32 = jnp.float32
BF16 = jnp.bfloat16
RANK = 4
ROWS = 16
LANES = 128
COLS = (28672, 28672, 8192)
BLOCK = 4 * LANES
PIECE = 4096
CHIPS = 64
BLOCK_ROWS = 17
HALF_BLOCKS = tuple(c // 2 // BLOCK for c in COLS)
FIRST_BLOCK = (0, HALF_BLOCKS[0], HALF_BLOCKS[0] + HALF_BLOCKS[1])


def lane_iota(rows):
    return lax.broadcasted_iota(jnp.int32, (rows, LANES), 1)


def merge_kernel(*refs):
    grads, errors, rights = refs[0:3], refs[3:6], refs[6:9]
    merged, partial = refs[9:12], refs[12]
    gbuf, ebuf, rbuf, sems = refs[13:16], refs[16:19], refs[19:22], refs[22]
    copies = []
    index = 0
    for m in range(3):
        for piece in range(COLS[m] // PIECE):
            cols = pl.ds(piece * PIECE, PIECE)
            group = [
                pltpu.make_async_copy(grads[m].at[0, :, cols], gbuf[m].at[:, cols], sems.at[index, 0]),
                pltpu.make_async_copy(errors[m].at[0, :, cols], ebuf[m].at[:, cols], sems.at[index, 1]),
                pltpu.make_async_copy(rights[m].at[:, cols], rbuf[m].at[:, cols], sems.at[index, 2]),
            ]
            for copy in group:
                copy.start()
            copies.append((m, piece, group))
            index += 1
    lanes = lane_iota(ROWS)
    result = jnp.zeros((ROWS, LANES), F32)
    totals = None
    for m, piece, group in copies:
        if piece == 0:
            totals = tuple(jnp.zeros((ROWS, LANES), F32) for _ in range(RANK))
        for copy in group:
            copy.wait()

        def step(j, acc, m=m, piece=piece):
            cols = pl.ds(pl.multiple_of(piece * PIECE + j * LANES, LANES), LANES)
            value = gbuf[m][:, cols] + ebuf[m][:, cols].astype(F32)
            merged[m][:, cols] = value
            return tuple(acc[i] + value * rbuf[m][i : i + 1, cols] for i in range(RANK))

        totals = lax.fori_loop(0, PIECE // LANES, step, totals, unroll=4)
        if piece == COLS[m] // PIECE - 1:
            for i in range(RANK):
                column = jnp.sum(totals[i], axis=1, keepdims=True)
                result = jnp.where(lanes == m * RANK + i, column, result)
    for k in range(8):
        partial[k] = result


def sum_replicas(gathered):
    return (
        ((gathered[0] + gathered[1]) + (gathered[2] + gathered[3]))
        + ((gathered[4] + gathered[5]) + (gathered[6] + gathered[7]))
    ) * 0.125


def fold(a, b, distance):
    mask = (lax.broadcasted_iota(jnp.int32, (8, LANES), 0) & distance) == 0
    return jnp.where(mask, a, b) + pltpu.roll(jnp.where(mask, b, a), 8 - distance, 0)


def product_kernel(own, gathered, *refs):
    merged, out = refs[0:3], refs[3]
    core = lax.rem(lax.axis_index("dp"), 2)
    half = core if own else 1 - core
    left = sum_replicas(gathered)
    lanes = lane_iota(1)
    gram = jnp.zeros((1, LANES), F32)
    for shift in range(RANK):
        other = left if shift == 0 else pltpu.roll(left, LANES - shift, 1)
        row = jnp.where(lanes < 3 * RANK, jnp.sum(left * other, axis=0, keepdims=True), 0.0)
        gram = gram + (row if shift == 0 else pltpu.roll(row, 16 * shift, 1))
    for m in range(3):
        columns = [
            jnp.broadcast_to(left[:, m * RANK + i : m * RANK + i + 1], (ROWS, LANES)) for i in range(RANK)
        ]

        def step(block, carry, m=m, columns=columns):
            first = half * (COLS[m] // 2) + block * BLOCK
            row = (FIRST_BLOCK[m] + block) * BLOCK_ROWS
            for pair in range(2):
                terms = []
                for b in range(2):
                    cols = pl.ds(pl.multiple_of(first + (2 * pair + b) * LANES, LANES), LANES)
                    value = merged[m][:, cols]
                    for i in range(RANK):
                        product = columns[i] * value
                        terms.append(product[:8] + product[8:])
                ones = [fold(terms[2 * k], terms[2 * k + 1], 1) for k in range(4)]
                twos = [fold(ones[2 * k], ones[2 * k + 1], 2) for k in range(2)]
                out[pl.ds(row + 8 * pair, 8), :] = fold(twos[0], twos[1], 4)
            out[pl.ds(row + 16, 1), :] = gram
            return carry

        lax.fori_loop(0, HALF_BLOCKS[m], step, 0, unroll=2)


def solve_kernel(blocks, gathered, copies, left_out, scratch):
    total = [jnp.zeros((16, LANES), F32) for _ in range(4)]
    grams = [jnp.zeros((1, LANES), F32) for _ in range(4)]
    for k in range(CHIPS):
        total[k % 4] = total[k % 4] + blocks[k * BLOCK_ROWS : k * BLOCK_ROWS + 16, :]
        grams[k % 4] = grams[k % 4] + blocks[k * BLOCK_ROWS + 16 : k * BLOCK_ROWS + 17, :]
    scratch[...] = (total[0] + total[1]) + (total[2] + total[3])
    gram = ((grams[0] + grams[1]) + (grams[2] + grams[3])) * 0.125

    def entry(i, j):
        shift = 16 * (i - j) + j
        return gram if shift == 0 else pltpu.roll(gram, LANES - shift, 1)

    factor = {}
    for j in range(RANK):
        for i in range(j, RANK):
            value = entry(i, j)
            for k in range(j):
                value = value - factor[i, k] * factor[j, k]
            factor[i, j] = jnp.sqrt(value) if i == j else value / factor[j, j]

    left_sum = sum_replicas(gathered)
    lanes = lane_iota(ROWS)
    valid = (lanes < 3 * RANK) & ((lanes & 3) == 0)
    rows, left = [], jnp.zeros((ROWS, LANES), F32)
    for i in range(RANK):
        current = left_sum if i == 0 else pltpu.roll(left_sum, LANES - i, 1)
        for j in range(i):
            current = current - factor[i, j] * rows[j]
        rows.append(current / factor[i, i])
        kept = jnp.where(valid, rows[i], 0.0)
        left = left + (kept if i == 0 else pltpu.roll(kept, i, 1))
    left_out[...] = left

    mine = (lax.axis_index("dp") // 2) * 16 + lax.axis_index("tensor")
    matrix = jnp.where(mine < FIRST_BLOCK[1], 0, jnp.where(mine < FIRST_BLOCK[2], 1, 2))
    one_lane = lane_iota(1) == matrix * RANK
    nexts = []
    for i in range(RANK):
        current = scratch[pl.ds(i, 4, stride=4), :] * 0.125
        for j in range(i):
            value = jnp.sum(jnp.where(one_lane, factor[i, j], 0.0), axis=1, keepdims=True)
            current = current - value * nexts[j]
        value = jnp.sum(jnp.where(one_lane, factor[i, i], 0.0), axis=1, keepdims=True)
        nexts.append(current / value)
    for i in range(RANK):
        scratch[pl.ds(i, 4, stride=4), :] = nexts[i]
    block = scratch[...]
    for k in range(CHIPS):
        copies[k] = block


OUT_PIECES = (4, 4, 1)


def finish_kernel(own, *refs):
    if own:
        rows, left_ref = refs[0:2]
        merged = refs[2:5]
        nexts, errors, lefts = refs[5:8], refs[8:11], refs[11:14]
        nbuf, ebuf, square, sems = refs[14:17], refs[17:20], refs[20], refs[21]
    else:
        rows, left_ref = refs[0:2]
        merged = refs[2:5]
        nexts, errors = refs[11:14], refs[14:17]
        nbuf, ebuf, sems = refs[17:20], refs[20:23], refs[23]
    core = lax.rem(lax.axis_index("dp"), 2)
    half = core if own else 1 - core
    left = left_ref[...]
    copies = []
    index = 0
    for m in range(3):
        size = COLS[m] // 2 // OUT_PIECES[m]
        columns = [
            jnp.broadcast_to(left[:, m * RANK + i : m * RANK + i + 1], (ROWS, LANES)) for i in range(RANK)
        ]
        for piece in range(OUT_PIECES[m]):

            def step(j, carry, m=m, piece=piece, columns=columns, size=size):
                local = pl.multiple_of(piece * size + j * LANES, LANES)
                value = merged[m][:, pl.ds(pl.multiple_of(half * (COLS[m] // 2) + local, LANES), LANES)]
                row = FIRST_BLOCK[m] * 16 + piece * (size // LANES) * RANK + j * RANK
                nbuf[m][:, pl.ds(local, LANES)] = rows[pl.ds(row, RANK), :]
                approx = columns[0] * rows[pl.ds(row, 1), :]
                for i in range(1, RANK):
                    approx = approx + columns[i] * rows[pl.ds(row + i, 1), :]
                ebuf[m][:, pl.ds(local, LANES)] = (value - approx).astype(BF16)
                return carry

            lax.fori_loop(0, size // LANES, step, 0, unroll=4)
            here = pl.ds(piece * size, size)
            there = pl.ds(pl.multiple_of(half * (COLS[m] // 2) + piece * size, LANES), size)
            for copy in (
                pltpu.make_async_copy(ebuf[m].at[:, here], errors[m].at[0, :, there], sems.at[index, 0]),
                pltpu.make_async_copy(nbuf[m].at[:, here], nexts[m].at[:, there], sems.at[index, 1]),
            ):
                copy.start()
                copies.append(copy)
            index += 1
    if own:
        square[...] = jnp.zeros((LANES, LANES), F32)
        square[0:ROWS, :] = left
        turned = square[...].T
        for m in range(3):
            lefts[m][...] = turned[m * RANK : (m + 1) * RANK, 0:ROWS]
    for copy in copies:
        copy.wait()


ANY = pl.BlockSpec(memory_space=pl.ANY)
VMEM = pl.BlockSpec(memory_space=pltpu.VMEM)
PARAMS = pltpu.CompilerParams(vmem_limit_bytes=24 * 2**20)


def cost(flops, size):
    return pl.CostEstimate(flops=flops, bytes_accessed=size, transcendentals=0)


def per_device(*args):
    grads, errors, rights = args[0:3], args[3:6], args[6:9]
    pieces = sum(COLS) // PIECE
    *merged, partial = pl.pallas_call(
        merge_kernel,
        out_shape=[pltpu.VMEM((ROWS, c), F32) for c in COLS] + [jax.ShapeDtypeStruct((8, ROWS, LANES), F32)],
        in_specs=[ANY] * 9,
        out_specs=[VMEM] * 4,
        scratch_shapes=[pltpu.VMEM((ROWS, c), F32) for c in COLS]
        + [pltpu.VMEM((ROWS, c), BF16) for c in COLS]
        + [pltpu.VMEM((RANK, c), F32) for c in COLS]
        + [pltpu.SemaphoreType.DMA((pieces, 3))],
        compiler_params=PARAMS,
        cost_estimate=cost(10**7, 7 * 2**20),
    )(*grads, *errors, *rights)
    gathered = lax.all_to_all(partial, "dp", 0, 0, tiled=True)

    rows = CHIPS * BLOCK_ROWS

    def product(own):
        return pl.pallas_call(
            functools.partial(product_kernel, own),
            out_shape=jax.ShapeDtypeStruct((rows, LANES), F32),
            in_specs=[VMEM] * 4,
            out_specs=VMEM,
            compiler_params=PARAMS,
            cost_estimate=cost(10**7, 5 * 2**20),
        )(gathered, *merged)

    swap = [(i, i ^ 1) for i in range(8)]
    sent = product(False)
    received = lax.ppermute(sent, "dp", swap)
    chip_sum = product(True) + received
    both = ("dp", "tensor")
    chips = [[(2 * x + core) * 16 + t for x in range(4) for t in range(16)] for core in range(2)]
    blocks = lax.all_to_all(
        chip_sum.reshape(CHIPS, 1, BLOCK_ROWS * LANES), both, 0, 0, tiled=True, axis_index_groups=chips
    ).reshape(rows, LANES)

    copies, left = pl.pallas_call(
        solve_kernel,
        out_shape=[
            jax.ShapeDtypeStruct((CHIPS, 16, LANES), F32),
            jax.ShapeDtypeStruct((ROWS, LANES), F32),
        ],
        in_specs=[VMEM] * 2,
        out_specs=[VMEM] * 2,
        scratch_shapes=[pltpu.VMEM((16, LANES), F32)],
        compiler_params=PARAMS,
        cost_estimate=cost(10**6, 2**20),
    )(blocks, gathered)
    mine = lax.all_to_all(copies, both, 0, 0, tiled=True, axis_index_groups=chips).reshape(CHIPS * 16, LANES)
    theirs = lax.ppermute(mine, "dp", swap)

    next_shapes = [jax.ShapeDtypeStruct((RANK, c), F32) for c in COLS]
    error_shapes = [jax.ShapeDtypeStruct((1, ROWS, c), BF16) for c in COLS]
    left_shapes = [jax.ShapeDtypeStruct((RANK, ROWS), F32)] * 3
    scratch = [pltpu.VMEM((RANK, c // 2), F32) for c in COLS] + [pltpu.VMEM((ROWS, c // 2), BF16) for c in COLS]
    sems = pltpu.SemaphoreType.DMA((sum(OUT_PIECES), 2))
    first = pl.pallas_call(
        functools.partial(finish_kernel, True),
        out_shape=next_shapes + error_shapes + left_shapes,
        in_specs=[VMEM] * 5,
        out_specs=[ANY] * 6 + [VMEM] * 3,
        scratch_shapes=scratch + [pltpu.VMEM((LANES, LANES), F32), sems],
        compiler_params=PARAMS,
        cost_estimate=cost(10**7, 4 * 2**20),
    )(mine, left, *merged)
    lefts = first[6:9]
    second = pl.pallas_call(
        functools.partial(finish_kernel, False),
        out_shape=next_shapes + error_shapes,
        in_specs=[VMEM] * 5 + [ANY] * 6,
        out_specs=[ANY] * 6,
        scratch_shapes=scratch + [sems],
        input_output_aliases={5 + k: k for k in range(6)},
        compiler_params=PARAMS,
        cost_estimate=cost(10**7, 4 * 2**20),
    )(theirs, left, *merged, *first[0:6])
    return (*lefts, *second)


def solution(mesh):
    cut = P("dp", "tensor", None)
    return jax.shard_map(
        per_device,
        mesh=mesh,
        in_specs=(cut,) * 6 + (P(),) * 3,
        out_specs=(P(None, "tensor"),) * 3 + (P(),) * 3 + (cut,) * 3,
        check_vma=False,
    )
```

time: 488 us -> 77.5 us (0.16)
  waiting for transfers between devices: 195 us -> 0.13 us
  blocking collectives: 228 us -> 47.4 us
  matrix products: 27.7 us -> 0 us
  between operations: 22.6 us -> 0.72 us
  Pallas kernels: 0 us -> 14.3 us
  other arithmetic: 11.7 us -> 0.06 us
  local copies, waits for them, and re-layouts: 1.06 us -> 10.3 us
    psum x8 -> x0, blocking collectives: 228 us -> none  [the longest x4 129 us: per_device(): lengths = lax.psum((squares[0], squares[1], squares[2]), 'tensor')]
    psum x2 -> x0, waiting for transfers between devices: 195 us -> none  [the longest x1 131 us: per_device(): across = lax.psum((terms[0], terms[1], terms[2]), 'tensor')]
    all_to_all x0 -> x3, blocking collectives: none -> 47.4 us  [the longest x1 21.4 us: per_device(): lax.all_to_all(chip_sum.reshape(CHIPS, 1, BLOCK_ROWS * LANES), both, 0, 0...]
    dot_general x21 -> x0, matrix products: 27.7 us -> none  [the longest x3 7.8 us: per_device(): lax.dot_general(bases[m_index], nexts[m_index], (((0,), (0,)), ((), ())),...]
    pallas_call x0 -> x6, Pallas kernels: none -> 14.3 us  [the longest x1 6.26 us: per_device(): pl.pallas_call(merge_kernel, out_shape=[pltpu.VMEM((ROWS, c), F32) for c...]
    unnamed x32 -> x18, local copies, waits for them, and re-layouts: 1.06 us -> 10.3 us
    reduce_sum x6 -> x0, other arithmetic: 5.54 us -> none  [per_device(): squares = [jnp.sum(item * item) for item in current]]
  transfers between devices with their start and end apart: 2 -> 2, of which waited for: 2 -> 1; matrix products, arithmetic and copies ran while one was open for 0% -> 0% of each run, Pallas kernels for 0% -> 5%
where the time goes in v1:
time: 77.5 us; the launch traced here: 77 us
  blocking collectives  47.4 us (61%)
  Pallas kernels  14.3 us (18%)
  local copies, waits for them, and re-layouts  10.3 us (13%)
  starting transfers between devices  4.16 us (5%)
    all_to_all x1, blocking collectives, per_device(): lax.all_to_all(chip_sum.reshape(CHIPS, 1, BLOCK_ROWS * LANES), both, 0, 0...  21.4 us
    all_to_all x1, blocking collectives, per_device(): lax.all_to_all(copies, both, 0, 0, tiled=True, axis_index_groups=chips)  15.6 us
    all_to_all x1, blocking collectives, per_device(): gathered = lax.all_to_all(partial, 'dp', 0, 0, tiled=True)  10.4 us
    unnamed x18, local copies, waits for them, and re-layouts  10.3 us
    pallas_call x1, Pallas kernels, per_device(): pl.pallas_call(merge_kernel, out_shape=[pltpu.VMEM((ROWS, c), F32) for c...  6.26 us
    ppermute x1, starting transfers between devices, per_device(): theirs = lax.ppermute(mine, 'dp', swap)  3.3 us
    pallas_call x2, Pallas kernels, product(): pl.pallas_call(functools.partial(product_kernel, own), out_shape=jax.Shap...  2.9 us
    pallas_call x1, Pallas kernels, per_device(): pl.pallas_call(functools.partial(finish_kernel, True), out_shape=next_sha...  2.7 us
  transfers between devices with their start and end apart: 2, of which 1 were waited for; matrix products, arithmetic and copies ran while one was open for 0% of the time, Pallas kernels for 5%

profile of v1, /device:TPU:1, one launch (start us, length us, event | category | flops | bytes accessed | tf_op | source)
XLA Modules:
  0.0 77.0 jit_solution(17378188917796118881)
XLA Ops:
  0.6 0.0 copy-start
  0.7 1.5 %copy-done = f32[1,16,28672]{2,1,0:T(8,128)S(1)} copy-done((f32[1,16,28672]{2,1,0:T(8,128)S(1)}, f32[1,16,28672]{2,1,0:T(8,128)}, u32[]{:S(2)}) %copy-start) | copy-done | bytes 1835032
  2.1 1.5 %copy-done.1 = f32[1,16,28672]{2,1,0:T(8,128)S(1)} copy-done((f32[1,16,28672]{2,1,0:T(8,128)S(1)}, f32[1,16,28672]{2,1,0:T(8,128)}, u32[]{:S(2)}) %copy-start.1) | copy-done | bytes 1835032
  3.6 1.2 %copy-done.2 = bf16[1,16,28672]{2,1,0:T(8,128)(2,1)S(1)} copy-done((bf16[1,16,28672]{2,1,0:T(8,128)(2,1)S(1)}, bf16[1,16,28672]{2,1,0:T(8,128)(2,1)}, u32[]{:S(2)}) %copy-start.2) | copy-done | bytes 917528
  4.8 1.2 %copy-done.3 = bf16[1,16,28672]{2,1,0:T(8,128)(2,1)S(1)} copy-done((bf16[1,16,28672]{2,1,0:T(8,128)(2,1)S(1)}, bf16[1,16,28672]{2,1,0:T(8,128)(2,1)}, u32[]{:S(2)}) %copy-start.3) | copy-done | bytes 917528
  6.0 1.0 %copy-done.4 = f32[1,16,8192]{2,1,0:T(8,128)S(1)} copy-done((f32[1,16,8192]{2,1,0:T(8,128)S(1)}, f32[1,16,8192]{2,1,0:T(8,128)}, u32[]{:S(2)}) %copy-start.4) | copy-done | bytes 524312
  7.0 1.0 %copy-done.5 = f32[4,28672]{1,0:T(4,128)S(1)} copy-done((f32[4,28672]{1,0:T(4,128)S(1)}, f32[4,28672]{1,0:T(4,128)}, u32[]{:S(2)}) %copy-start.5) | copy-done | bytes 458776
  8.1 1.0 %copy-done.6 = f32[4,28672]{1,0:T(4,128)S(1)} copy-done((f32[4,28672]{1,0:T(4,128)S(1)}, f32[4,28672]{1,0:T(4,128)}, u32[]{:S(2)}) %copy-start.6) | copy-done | bytes 458776
  9.1 0.9 %copy-done.7 = bf16[1,16,8192]{2,1,0:T(8,128)(2,1)S(1)} copy-done((bf16[1,16,8192]{2,1,0:T(8,128)(2,1)S(1)}, bf16[1,16,8192]{2,1,0:T(8,128)(2,1)}, u32[]{:S(2)}) %copy-start.7) | copy-done | bytes 262168
  10.0 0.9 %copy-done.8 = f32[4,8192]{1,0:T(4,128)S(1)} copy-done((f32[4,8192]{1,0:T(4,128)S(1)}, f32[4,8192]{1,0:T(4,128)}, u32[]{:S(2)}) %copy-start.8) | copy-done | bytes 131096
  10.9 6.3 %shard_map.160 = (f32[16,28672]{1,0:T(8,128)S(1)}, f32[16,28672]{1,0:T(8,128)S(1)}, f32[16,8192]{1,0:T(8,128)S(1)}, f32[8,16,128]{2,1,0:T(8,128)S(1)}) custom-call(f32[1,16,28672]{2,1,0:T(8,128)S(1)} %copy-done, f32[1,16,28672]{2,1,0:T(8,128)S(1)} %copy-done.1, f32[1,16,8192]{2,1,0:T(8,128)S(1)} %copy-done.4, bf16[1,16,28672]{2,1,0:T(8,128)(2,1)S(1)} %copy-done.2, ...), custom_call_target="tpu_custom_call" | custom-call | flops 10000000 | bytes 7340032 | tf_op jit(solution)/shard_map/pallas_call | solution.py:239
  17.2 10.4 %all_to_all.15.gathered = f32[8,16,128]{2,1,0:T(8,128)S(1)} all-to-all(f32[8,16,128]{2,1,0:T(8,128)S(1)} %get-tuple-element.30), channel_id=1, replica_groups=mesh['dp'=8,'tensor'=16] {'dp'}, dimensions={0} | all-to-all | bytes 131072 | tf_op jit(solution)/shard_map/all_to_all | solution.py:251
  27.7 1.4 %shard_map.162 = f32[1088,128]{1,0:T(8,128)S(1)} custom-call(f32[8,16,128]{2,1,0:T(8,128)S(1)} %all_to_all.15.gathered, f32[16,28672]{1,0:T(8,128)S(1)} %get-tuple-element.31.refs_0_.refs_2_, f32[16,28672]{1,0:T(8,128)S(1)} %get-tuple-element.32.refs_1_.refs_3_, f32[16,8192]{1,0:T(8,128)S(1)} %get-tuple-element.33.refs_2_.refs_4_), custom_call_target="tpu_custom_call" | custom-call | flops 10000000 | bytes 5242880 | tf_op jit(solution)/shard_map/pallas_call | solution.py:256
  29.1 0.9 %collective-permute-start = (f32[1088,128]{1,0:T(8,128)S(1)}, f32[1088,128]{1,0:T(8,128)S(1)}, u32[]{:S(2)}, u32[]{:S(2)}) collective-permute-start(f32[1088,128]{1,0:T(8,128)S(1)} %shard_map.162), channel_id=1, source_target_pairs={{0,16},{16,0},{32,48},{48,32},{64,80},{80,64},{96,112},{112,96},{1... | collective-permute-start | bytes 1671176 | tf_op jit(solution)/shard_map/ppermute | solution.py:267
  30.0 1.4 %shard_map.161 = f32[1088,128]{1,0:T(8,128)S(1)} custom-call(f32[8,16,128]{2,1,0:T(8,128)S(1)} %all_to_all.15.gathered, f32[16,28672]{1,0:T(8,128)S(1)} %get-tuple-element.31.refs_0_.refs_2_, f32[16,28672]{1,0:T(8,128)S(1)} %get-tuple-element.32.refs_1_.refs_3_, f32[16,8192]{1,0:T(8,128)S(1)} %get-tuple-element.33.refs_2_.refs_4_), custom_call_target="tpu_custom_call" | custom-call | flops 10000000 | bytes 5242880 | tf_op jit(solution)/shard_map/pallas_call | solution.py:256
  31.4 0.1 collective-permute-done
  31.6 0.1 add.3
  31.6 21.4 %all_to_all.16 = f32[64,1,2176]{2,1,0:T(1,128)S(1)} all-to-all(f32[64,1,2176]{2,1,0:T(1,128)S(1)} %bitcast.6), channel_id=1, replica_groups={{0,1,2,3,4,5,6,7,8,9,10,11,12,13,14,15,32,33,34,35,36,37,38,39,40,41,42..., dimensions={0} | all-to-all | bytes 1114112 | tf_op jit(solution)/shard_map/all_to_all | solution.py:271
  53.0 0.3 shard_map.163
  53.3 15.6 %all_to_all.17 = f32[64,16,128]{2,1,0:T(8,128)S(1)} all-to-all(f32[64,16,128]{2,1,0:T(8,128)S(1)} %get-tuple-element.34), channel_id=1, replica_groups={{0,1,2,3,4,5,6,7,8,9,10,11,12,13,14,15,32,33,34,35,36,37,38,39,40,41,42..., dimensions={0} | all-to-all | bytes 1048576 | tf_op jit(solution)/shard_map/all_to_all | solution.py:287
  68.8 3.3 %collective-permute-start.1 = (f32[1024,128]{1,0:T(8,128)S(1)}, f32[1024,128]{1,0:T(8,128)S(1)}, u32[]{:S(2)}, u32[]{:S(2)}) collective-permute-start(f32[1024,128]{1,0:T(8,128)S(1)} %bitcast.4), channel_id=1, source_target_pairs={{0,16},{16,0},{32,48},{48,32},{64,80},{80,64},{96,112},{112,96},{1... | collective-permute-start | bytes 1572872 | tf_op jit(solution)/shard_map/ppermute | solution.py:288
  72.1 2.7 %shard_map.164 = (f32[4,28672]{1,0:T(4,128)}, f32[4,28672]{1,0:T(4,128)}, f32[4,8192]{1,0:T(4,128)}, bf16[1,16,28672]{2,1,0:T(8,128)(2,1)}, bf16[1,16,28672]{2,1...) custom-call(f32[1024,128]{1,0:T(8,128)S(1)} %bitcast.5, ...), custom_call_target="tpu_custom_call" | custom-call | flops 10000000 | bytes 4194304 | tf_op jit(solution)/shard_map/pallas_call | solution.py:295
  74.9 0.0 collective-permute-done.1.refs_0_
  74.9 2.1 %shard_map.165 = (f32[4,28672]{1,0:T(4,128)}, f32[4,28672]{1,0:T(4,128)}, f32[4,8192]{1,0:T(4,128)}, bf16[1,16,28672]{2,1,0:T(8,128)(2,1)}, bf16[1,16,28672]{2,1,0:T(8,128)(2,1)}, /*index=5*/bf16[1,16,8192]{2,1,0:T(8,128)(2,1)}) custom-call(f32[1024,128]{1,0:T(8,128)S(1)} %collective-permute-done, ...), custom_call_target="tpu_custom_call", output_to_operand_aliasing={{0}: (5, {}), {1}: (6, {}), {2}: (7, {}), {3}: (8, {}), {4}... | custom-call | flops 10000000 | bytes 4194304 | tf_op jit(solution)/shard_map/pallas_call | solution.py:305
  (8 shorter events, 0.0 us)
Async XLA Ops:
  0.6 1.5 %copy-start = (f32[1,16,28672]{2,1,0:T(8,128)S(1)}, f32[1,16,28672]{2,1,0:T(8,128)}, u32[]{:S(2)}) copy-start(f32[1,16,28672]{2,1,0:T(8,128)} %refs_0_.1) | copy-start | bytes 5505028
  2.1 1.5 %copy-start.1 = (f32[1,16,28672]{2,1,0:T(8,128)S(1)}, f32[1,16,28672]{2,1,0:T(8,128)}, u32[]{:S(2)}) copy-start(f32[1,16,28672]{2,1,0:T(8,128)} %refs_1_.1) | copy-start | bytes 5505028
  3.6 1.2 %copy-start.2 = (bf16[1,16,28672]{2,1,0:T(8,128)(2,1)S(1)}, bf16[1,16,28672]{2,1,0:T(8,128)(2,1)}, u32[]{:S(2)}) copy-start(bf16[1,16,28672]{2,1,0:T(8,128)(2,1)} %refs_3_.1) | copy-start | bytes 2752516
  4.8 1.2 %copy-start.3 = (bf16[1,16,28672]{2,1,0:T(8,128)(2,1)S(1)}, bf16[1,16,28672]{2,1,0:T(8,128)(2,1)}, u32[]{:S(2)}) copy-start(bf16[1,16,28672]{2,1,0:T(8,128)(2,1)} %refs_4_.1) | copy-start | bytes 2752516
  6.0 1.0 %copy-start.4 = (f32[1,16,8192]{2,1,0:T(8,128)S(1)}, f32[1,16,8192]{2,1,0:T(8,128)}, u32[]{:S(2)}) copy-start(f32[1,16,8192]{2,1,0:T(8,128)} %refs_2_.1) | copy-start | bytes 1572868
  7.0 1.0 %copy-start.5 = (f32[4,28672]{1,0:T(4,128)S(1)}, f32[4,28672]{1,0:T(4,128)}, u32[]{:S(2)}) copy-start(f32[4,28672]{1,0:T(4,128)} %refs_6_.1) | copy-start | bytes 1376260
  8.1 1.0 %copy-start.6 = (f32[4,28672]{1,0:T(4,128)S(1)}, f32[4,28672]{1,0:T(4,128)}, u32[]{:S(2)}) copy-start(f32[4,28672]{1,0:T(4,128)} %refs_7_.1) | copy-start | bytes 1376260
  9.1 0.9 %copy-start.7 = (bf16[1,16,8192]{2,1,0:T(8,128)(2,1)S(1)}, bf16[1,16,8192]{2,1,0:T(8,128)(2,1)}, u32[]{:S(2)}) copy-start(bf16[1,16,8192]{2,1,0:T(8,128)(2,1)} %refs_5_.1) | copy-start | bytes 786436
  10.0 0.9 %copy-start.8 = (f32[4,8192]{1,0:T(4,128)S(1)}, f32[4,8192]{1,0:T(4,128)}, u32[]{:S(2)}) copy-start(f32[4,8192]{1,0:T(4,128)} %refs_8_.1) | copy-start | bytes 393220
  29.1 2.4 %collective-permute-start = (f32[1088,128]{1,0:T(8,128)S(1)}, f32[1088,128]{1,0:T(8,128)S(1)}, u32[]{:S(2)}, u32[]{:S(2)}) collective-permute-start(f32[1088,128]{1,0:T(8,128)S(1)} %shard_map.162), channel_id=1, source_target_pairs={{0,16},{16,0},{32,48},{48,32},{64,80},{80,64},{96,112},{112,96},{1... | collective-permute-start | bytes 1671176 | tf_op jit(solution)/shard_map/ppermute | solution.py:267
  68.8 6.0 %collective-permute-start.1 = (f32[1024,128]{1,0:T(8,128)S(1)}, f32[1024,128]{1,0:T(8,128)S(1)}, u32[]{:S(2)}, u32[]{:S(2)}) collective-permute-start(f32[1024,128]{1,0:T(8,128)S(1)} %bitcast.4), channel_id=1, source_target_pairs={{0,16},{16,0},{32,48},{48,32},{64,80},{80,64},{96,112},{112,96},{1... | collective-permute-start | bytes 1572872 | tf_op jit(solution)/shard_map/ppermute | solution.py:288

commit v2 on v1

--- a/solution.py
+++ b/solution.py
@@ -37,8 +37,9 @@
             group = [
                 pltpu.make_async_copy(grads[m].at[0, :, cols], gbuf[m].at[:, cols], sems.at[index, 0]),
                 pltpu.make_async_copy(errors[m].at[0, :, cols], ebuf[m].at[:, cols], sems.at[index, 1]),
-                pltpu.make_async_copy(rights[m].at[:, cols], rbuf[m].at[:, cols], sems.at[index, 2]),
             ]
+            if piece == 0:
+                group.append(pltpu.make_async_copy(rights[m], rbuf[m], sems.at[index, 2]))
             for copy in group:
                 copy.start()
             copies.append((m, piece, group))
@@ -58,7 +59,7 @@
             merged[m][:, cols] = value
             return tuple(acc[i] + value * rbuf[m][i : i + 1, cols] for i in range(RANK))
 
-        totals = lax.fori_loop(0, PIECE // LANES, step, totals, unroll=4)
+        totals = lax.fori_loop(0, PIECE // LANES, step, totals, unroll=8)
         if piece == COLS[m] // PIECE - 1:
             for i in range(RANK):
                 column = jnp.sum(totals[i], axis=1, keepdims=True)
@@ -204,7 +205,7 @@
                 ebuf[m][:, pl.ds(local, LANES)] = (value - approx).astype(BF16)
                 return carry
 
-            lax.fori_loop(0, size // LANES, step, 0, unroll=4)
+            lax.fori_loop(0, size // LANES, step, 0, unroll=14 if m < 2 else 16)
             here = pl.ds(piece * size, size)
             there = pl.ds(pl.multiple_of(half * (COLS[m] // 2) + piece * size, LANES), size)
             for copy in (
@@ -236,10 +237,11 @@
 def per_device(*args):
     grads, errors, rights = args[0:3], args[3:6], args[6:9]
     pieces = sum(COLS) // PIECE
+    grads, errors, rights = ([pltpu.with_memory_space_constraint(x, pltpu.HBM) for x in group] for group in (grads, errors, rights))
     *merged, partial = pl.pallas_call(
         merge_kernel,
         out_shape=[pltpu.VMEM((ROWS, c), F32) for c in COLS] + [jax.ShapeDtypeStruct((8, ROWS, LANES), F32)],
-        in_specs=[ANY] * 9,
+        in_specs=[pl.BlockSpec(memory_space=pltpu.HBM)] * 9,
         out_specs=[VMEM] * 4,
         scratch_shapes=[pltpu.VMEM((ROWS, c), F32) for c in COLS]
         + [pltpu.VMEM((ROWS, c), BF16) for c in COLS]

time: 77.5 us -> 64.2 us (0.83)
  local copies, waits for them, and re-layouts: 10.3 us -> 0 us
  Pallas kernels: 14.3 us -> 11.5 us
    unnamed x18 -> x0, local copies, waits for them, and re-layouts: 10.3 us -> none
    pallas_call x1, Pallas kernels: 6.26 us -> 4.08 us  [per_device(): pl.pallas_call(merge_kernel, out_shape=[pltpu.VMEM((ROWS, c), F32) for c...]
  transfers between devices with their start and end apart: 2 -> 2, of which waited for: 1 -> 1; matrix products, arithmetic and copies ran while one was open for 0% -> 0% of each run, Pallas kernels for 5% -> 6%
where the time goes in v2:
time: 64.2 us; the launch traced here: 63.9 us
  blocking collectives  47.4 us (74%)
  Pallas kernels  11.5 us (18%)
  starting transfers between devices  4.16 us (6%)
  between operations  0.7 us (1%)
    all_to_all x1, blocking collectives, per_device(): lax.all_to_all(chip_sum.reshape(CHIPS, 1, BLOCK_ROWS * LANES), both, 0, 0...  21.4 us
    all_to_all x1, blocking collectives, per_device(): lax.all_to_all(copies, both, 0, 0, tiled=True, axis_index_groups=chips)  15.6 us
    all_to_all x1, blocking collectives, per_device(): gathered = lax.all_to_all(partial, 'dp', 0, 0, tiled=True)  10.4 us
    pallas_call x1, Pallas kernels, per_device(): pl.pallas_call(merge_kernel, out_shape=[pltpu.VMEM((ROWS, c), F32) for c...  4.08 us
    ppermute x1, starting transfers between devices, per_device(): theirs = lax.ppermute(mine, 'dp', swap)  3.3 us
    pallas_call x2, Pallas kernels, product(): pl.pallas_call(functools.partial(product_kernel, own), out_shape=jax.Shap...  2.9 us
    pallas_call x1, Pallas kernels, per_device(): pl.pallas_call(functools.partial(finish_kernel, True), out_shape=next_sha...  2.41 us
    pallas_call x1, Pallas kernels, per_device(): pl.pallas_call(functools.partial(finish_kernel, False), out_shape=next_sh...  1.84 us
  transfers between devices with their start and end apart: 2, of which 1 were waited for; matrix products, arithmetic and copies ran while one was open for 0% of the time, Pallas kernels for 6%

profile of v2, /device:TPU:1, one launch (start us, length us, event | category | flops | bytes accessed | tf_op | source)
XLA Modules:
  0.0 63.9 jit_solution(7458601602048527809)
XLA Ops:
  0.6 4.1 %shard_map.160 = (f32[16,28672]{1,0:T(8,128)S(1)}, f32[16,28672]{1,0:T(8,128)S(1)}, f32[16,8192]{1,0:T(8,128)S(1)}, f32[8,16,128]{2,1,0:T(8,128)S(1)}) custom-call(f32[1,16,28672]{2,1,0:T(8,128)} %refs_0_.1, f32[1,16,28672]{2,1,0:T(8,128)} %refs_1_.1, f32[1,16,8192]{2,1,0:T(8,128)} %refs_2_.1, bf16[1,16,28672]{2,1,0:T(8,128)(2,1)} %refs_3_.1, ...), custom_call_target="tpu_custom_call" | custom-call | flops 10000000 | bytes 7340032 | tf_op jit(solution)/shard_map/pallas_call | solution.py:241
  4.7 10.4 %all_to_all.15.gathered = f32[8,16,128]{2,1,0:T(8,128)S(1)} all-to-all(f32[8,16,128]{2,1,0:T(8,128)S(1)} %get-tuple-element.30), channel_id=1, replica_groups=mesh['dp'=8,'tensor'=16] {'dp'}, dimensions={0} | all-to-all | bytes 131072 | tf_op jit(solution)/shard_map/all_to_all | solution.py:253
  15.2 1.4 %shard_map.162 = f32[1088,128]{1,0:T(8,128)S(1)} custom-call(f32[8,16,128]{2,1,0:T(8,128)S(1)} %all_to_all.15.gathered, f32[16,28672]{1,0:T(8,128)S(1)} %get-tuple-element.31.refs_0_.refs_2_, f32[16,28672]{1,0:T(8,128)S(1)} %get-tuple-element.32.refs_1_.refs_3_, f32[16,8192]{1,0:T(8,128)S(1)} %get-tuple-element.33.refs_2_.refs_4_), custom_call_target="tpu_custom_call" | custom-call | flops 10000000 | bytes 5242880 | tf_op jit(solution)/shard_map/pallas_call | solution.py:258
  16.6 0.9 %collective-permute-start = (f32[1088,128]{1,0:T(8,128)S(1)}, f32[1088,128]{1,0:T(8,128)S(1)}, u32[]{:S(2)}, u32[]{:S(2)}) collective-permute-start(f32[1088,128]{1,0:T(8,128)S(1)} %shard_map.162), channel_id=1, source_target_pairs={{0,16},{16,0},{32,48},{48,32},{64,80},{80,64},{96,112},{112,96},{1... | collective-permute-start | bytes 1671176 | tf_op jit(solution)/shard_map/ppermute | solution.py:269
  17.5 1.4 %shard_map.161 = f32[1088,128]{1,0:T(8,128)S(1)} custom-call(f32[8,16,128]{2,1,0:T(8,128)S(1)} %all_to_all.15.gathered, f32[16,28672]{1,0:T(8,128)S(1)} %get-tuple-element.31.refs_0_.refs_2_, f32[16,28672]{1,0:T(8,128)S(1)} %get-tuple-element.32.refs_1_.refs_3_, f32[16,8192]{1,0:T(8,128)S(1)} %get-tuple-element.33.refs_2_.refs_4_), custom_call_target="tpu_custom_call" | custom-call | flops 10000000 | bytes 5242880 | tf_op jit(solution)/shard_map/pallas_call | solution.py:258
  19.0 0.1 collective-permute-done
  19.1 0.1 add.3
  19.1 21.4 %all_to_all.16 = f32[64,1,2176]{2,1,0:T(1,128)S(1)} all-to-all(f32[64,1,2176]{2,1,0:T(1,128)S(1)} %bitcast.6), channel_id=1, replica_groups={{0,1,2,3,4,5,6,7,8,9,10,11,12,13,14,15,32,33,34,35,36,37,38,39,40,41,42..., dimensions={0} | all-to-all | bytes 1114112 | tf_op jit(solution)/shard_map/all_to_all | solution.py:273
  40.5 0.3 shard_map.163
  40.8 15.6 %all_to_all.17 = f32[64,16,128]{2,1,0:T(8,128)S(1)} all-to-all(f32[64,16,128]{2,1,0:T(8,128)S(1)} %get-tuple-element.34), channel_id=1, replica_groups={{0,1,2,3,4,5,6,7,8,9,10,11,12,13,14,15,32,33,34,35,36,37,38,39,40,41,42..., dimensions={0} | all-to-all | bytes 1048576 | tf_op jit(solution)/shard_map/all_to_all | solution.py:289
  56.4 3.3 %collective-permute-start.1 = (f32[1024,128]{1,0:T(8,128)S(1)}, f32[1024,128]{1,0:T(8,128)S(1)}, u32[]{:S(2)}, u32[]{:S(2)}) collective-permute-start(f32[1024,128]{1,0:T(8,128)S(1)} %bitcast.4), channel_id=1, source_target_pairs={{0,16},{16,0},{32,48},{48,32},{64,80},{80,64},{96,112},{112,96},{1... | collective-permute-start | bytes 1572872 | tf_op jit(solution)/shard_map/ppermute | solution.py:290
  59.7 2.4 %shard_map.164 = (f32[4,28672]{1,0:T(4,128)}, f32[4,28672]{1,0:T(4,128)}, f32[4,8192]{1,0:T(4,128)}, bf16[1,16,28672]{2,1,0:T(8,128)(2,1)}, bf16[1,16,28672]{2,1...) custom-call(f32[1024,128]{1,0:T(8,128)S(1)} %bitcast.5, ...), custom_call_target="tpu_custom_call" | custom-call | flops 10000000 | bytes 4194304 | tf_op jit(solution)/shard_map/pallas_call | solution.py:297
  62.1 0.0 collective-permute-done.1.refs_0_
  62.1 1.8 %shard_map.165 = (f32[4,28672]{1,0:T(4,128)}, f32[4,28672]{1,0:T(4,128)}, f32[4,8192]{1,0:T(4,128)}, bf16[1,16,28672]{2,1,0:T(8,128)(2,1)}, bf16[1,16,28672]{2,1,0:T(8,128)(2,1)}, /*index=5*/bf16[1,16,8192]{2,1,0:T(8,128)(2,1)}) custom-call(f32[1024,128]{1,0:T(8,128)S(1)} %collective-permute-done, ...), custom_call_target="tpu_custom_call", output_to_operand_aliasing={{0}: (5, {}), {1}: (6, {}), {2}: (7, {}), {3}: (8, {}), {4}... | custom-call | flops 10000000 | bytes 4194304 | tf_op jit(solution)/shard_map/pallas_call | solution.py:307
Async XLA Ops:
  16.6 2.4 %collective-permute-start = (f32[1088,128]{1,0:T(8,128)S(1)}, f32[1088,128]{1,0:T(8,128)S(1)}, u32[]{:S(2)}, u32[]{:S(2)}) collective-permute-start(f32[1088,128]{1,0:T(8,128)S(1)} %shard_map.162), channel_id=1, source_target_pairs={{0,16},{16,0},{32,48},{48,32},{64,80},{80,64},{96,112},{112,96},{1... | collective-permute-start | bytes 1671176 | tf_op jit(solution)/shard_map/ppermute | solution.py:269
  56.4 5.7 %collective-permute-start.1 = (f32[1024,128]{1,0:T(8,128)S(1)}, f32[1024,128]{1,0:T(8,128)S(1)}, u32[]{:S(2)}, u32[]{:S(2)}) collective-permute-start(f32[1024,128]{1,0:T(8,128)S(1)} %bitcast.4), channel_id=1, source_target_pairs={{0,16},{16,0},{32,48},{48,32},{64,80},{80,64},{96,112},{112,96},{1... | collective-permute-start | bytes 1572872 | tf_op jit(solution)/shard_map/ppermute | solution.py:290

commit v3 on v2

--- a/solution.py
+++ b/solution.py
@@ -15,8 +15,9 @@
 COLS = (28672, 28672, 8192)
 BLOCK = 4 * LANES
 PIECE = 4096
-CHIPS = 64
-BLOCK_ROWS = 17
+GROUP = 8
+SHARE = 128
+SHARE_ROWS = SHARE + 1
 HALF_BLOCKS = tuple(c // 2 // BLOCK for c in COLS)
 FIRST_BLOCK = (0, HALF_BLOCKS[0], HALF_BLOCKS[0] + HALF_BLOCKS[1])
 
@@ -98,7 +99,8 @@
 
         def step(block, carry, m=m, columns=columns):
             first = half * (COLS[m] // 2) + block * BLOCK
-            row = (FIRST_BLOCK[m] + block) * BLOCK_ROWS
+            place = FIRST_BLOCK[m] + block
+            row = place * 16 + place // 8
             for pair in range(2):
                 terms = []
                 for b in range(2):
@@ -110,20 +112,30 @@
                 ones = [fold(terms[2 * k], terms[2 * k + 1], 1) for k in range(4)]
                 twos = [fold(ones[2 * k], ones[2 * k + 1], 2) for k in range(2)]
                 out[pl.ds(row + 8 * pair, 8), :] = fold(twos[0], twos[1], 4)
-            out[pl.ds(row + 16, 1), :] = gram
             return carry
 
         lax.fori_loop(0, HALF_BLOCKS[m], step, 0, unroll=2)
-
-
-def solve_kernel(blocks, gathered, copies, left_out, scratch):
-    total = [jnp.zeros((16, LANES), F32) for _ in range(4)]
-    grams = [jnp.zeros((1, LANES), F32) for _ in range(4)]
-    for k in range(CHIPS):
-        total[k % 4] = total[k % 4] + blocks[k * BLOCK_ROWS : k * BLOCK_ROWS + 16, :]
-        grams[k % 4] = grams[k % 4] + blocks[k * BLOCK_ROWS + 16 : k * BLOCK_ROWS + 17, :]
-    scratch[...] = (total[0] + total[1]) + (total[2] + total[3])
-    gram = ((grams[0] + grams[1]) + (grams[2] + grams[3])) * 0.125
+    for k in range(GROUP):
+        out[k * SHARE_ROWS + SHARE : (k + 1) * SHARE_ROWS, :] = gram
+
+
+def sum_shares(shares, start, rows):
+    parts = [shares[k * SHARE_ROWS + start : k * SHARE_ROWS + start + rows, :] for k in range(GROUP)]
+    return ((parts[0] + parts[1]) + (parts[2] + parts[3])) + ((parts[4] + parts[5]) + (parts[6] + parts[7]))
+
+
+def sum_kernel(shares, copies):
+    for start in range(0, SHARE_ROWS, 16):
+        rows = min(16, SHARE_ROWS - start)
+        total = sum_shares(shares, start, rows)
+        for k in range(GROUP):
+            copies[k * SHARE_ROWS + start : k * SHARE_ROWS + start + rows, :] = total
+
+
+def solve_kernel(shares, gathered, copies, left_out, scratch):
+    for start in range(0, SHARE, 16):
+        scratch[start : start + 16, :] = sum_shares(shares, start, 16)
+    gram = sum_shares(shares, SHARE, 1) * 0.125
 
     def entry(i, j):
         shift = 16 * (i - j) + j
@@ -150,22 +162,24 @@
         left = left + (kept if i == 0 else pltpu.roll(kept, i, 1))
     left_out[...] = left
 
-    mine = (lax.axis_index("dp") // 2) * 16 + lax.axis_index("tensor")
-    matrix = jnp.where(mine < FIRST_BLOCK[1], 0, jnp.where(mine < FIRST_BLOCK[2], 1, 2))
-    one_lane = lane_iota(1) == matrix * RANK
-    nexts = []
-    for i in range(RANK):
-        current = scratch[pl.ds(i, 4, stride=4), :] * 0.125
-        for j in range(i):
-            value = jnp.sum(jnp.where(one_lane, factor[i, j], 0.0), axis=1, keepdims=True)
-            current = current - value * nexts[j]
-        value = jnp.sum(jnp.where(one_lane, factor[i, i], 0.0), axis=1, keepdims=True)
-        nexts.append(current / value)
-    for i in range(RANK):
-        scratch[pl.ds(i, 4, stride=4), :] = nexts[i]
-    block = scratch[...]
-    for k in range(CHIPS):
-        copies[k] = block
+    dp, tensor = lax.axis_index("dp"), lax.axis_index("tensor")
+    place = (dp // 2 % 2) * 4 + (tensor // 4 % 2) * 2 + tensor % 2
+    for part in range(2):
+        first = (2 * place + part) * (SHARE // 2 // 16)
+        matrix = jnp.where(first < FIRST_BLOCK[1], 0, jnp.where(first < FIRST_BLOCK[2], 1, 2))
+        one_lane = lane_iota(1) == matrix * RANK
+        nexts = []
+        for i in range(RANK):
+            current = scratch[pl.ds(part * (SHARE // 2) + i, SHARE // 8, stride=RANK), :] * 0.125
+            for j in range(i):
+                value = jnp.sum(jnp.where(one_lane, factor[i, j], 0.0), axis=1, keepdims=True)
+                current = current - value * nexts[j]
+            value = jnp.sum(jnp.where(one_lane, factor[i, i], 0.0), axis=1, keepdims=True)
+            nexts.append(current / value)
+        for i in range(RANK):
+            scratch[pl.ds(part * (SHARE // 2) + i, SHARE // 8, stride=RANK), :] = nexts[i]
+    for k in range(GROUP):
+        copies[k] = scratch[...]
 
 
 OUT_PIECES = (4, 4, 1)
@@ -234,6 +248,20 @@
     return pl.CostEstimate(flops=flops, bytes_accessed=size, transcendentals=0)
 
 
+def groups():
+    at = {}
+    for x in range(4):
+        for core in range(2):
+            for z in range(4):
+                for y in range(4):
+                    place = (x % 2) * 4 + (z % 2) * 2 + y % 2
+                    cube = (x // 2) * 4 + (z // 2) * 2 + y // 2
+                    at[core, cube, place] = (2 * x + core) * 16 + z * 4 + y
+    cubes = [[at[core, cube, place] for place in range(8)] for core in range(2) for cube in range(8)]
+    peers = [[at[core, cube, place] for cube in range(8)] for core in range(2) for place in range(8)]
+    return cubes, peers
+
+
 def per_device(*args):
     grads, errors, rights = args[0:3], args[3:6], args[6:9]
     pieces = sum(COLS) // PIECE
@@ -252,7 +280,13 @@
     )(*grads, *errors, *rights)
     gathered = lax.all_to_all(partial, "dp", 0, 0, tiled=True)
 
-    rows = CHIPS * BLOCK_ROWS
+    rows = GROUP * SHARE_ROWS
+    both = ("dp", "tensor")
+    cubes, peers = groups()
+
+    def exchange(shares, members):
+        flat = shares.reshape(GROUP, 1, SHARE_ROWS * LANES)
+        return lax.all_to_all(flat, both, 0, 0, tiled=True, axis_index_groups=members).reshape(rows, LANES)
 
     def product(own):
         return pl.pallas_call(
@@ -268,25 +302,27 @@
     sent = product(False)
     received = lax.ppermute(sent, "dp", swap)
     chip_sum = product(True) + received
-    both = ("dp", "tensor")
-    chips = [[(2 * x + core) * 16 + t for x in range(4) for t in range(16)] for core in range(2)]
-    blocks = lax.all_to_all(
-        chip_sum.reshape(CHIPS, 1, BLOCK_ROWS * LANES), both, 0, 0, tiled=True, axis_index_groups=chips
-    ).reshape(rows, LANES)
-
+    cube_sums = pl.pallas_call(
+        sum_kernel,
+        out_shape=jax.ShapeDtypeStruct((rows, LANES), F32),
+        in_specs=[VMEM],
+        out_specs=VMEM,
+        compiler_params=PARAMS,
+        cost_estimate=cost(10**5, 2**20),
+    )(exchange(chip_sum, cubes))
     copies, left = pl.pallas_call(
         solve_kernel,
         out_shape=[
-            jax.ShapeDtypeStruct((CHIPS, 16, LANES), F32),
+            jax.ShapeDtypeStruct((GROUP, SHARE, LANES), F32),
             jax.ShapeDtypeStruct((ROWS, LANES), F32),
         ],
         in_specs=[VMEM] * 2,
         out_specs=[VMEM] * 2,
-        scratch_shapes=[pltpu.VMEM((16, LANES), F32)],
+        scratch_shapes=[pltpu.VMEM((SHARE, LANES), F32)],
         compiler_params=PARAMS,
         cost_estimate=cost(10**6, 2**20),
-    )(blocks, gathered)
-    mine = lax.all_to_all(copies, both, 0, 0, tiled=True, axis_index_groups=chips).reshape(CHIPS * 16, LANES)
+    )(exchange(cube_sums, peers), gathered)
+    mine = lax.all_to_all(copies, both, 0, 0, tiled=True, axis_index_groups=cubes).reshape(GROUP * SHARE, LANES)
     theirs = lax.ppermute(mine, "dp", swap)
 
     next_shapes = [jax.ShapeDtypeStruct((RANK, c), F32) for c in COLS]

time: 64.2 us -> 70.6 us (1.100)
  blocking collectives: 47.4 us -> 53 us
  starting transfers between devices: 4.16 us -> 4.88 us
    all_to_all x2 -> x3, blocking collectives: 36.9 us -> 42.5 us  [the longest x2 32.9 us: exchange(): lax.all_to_all(flat, both, 0, 0, tiled=True, axis_index_groups=members)]
    ppermute x1, starting transfers between devices: 3.3 us -> 4.02 us  [per_device(): theirs = lax.ppermute(mine, 'dp', swap)]
  transfers between devices with their start and end apart: 2 -> 2, of which waited for: 1 -> 0; matrix products, arithmetic and copies ran while one was open for 0% -> 0% of each run, Pallas kernels for 6% -> 6%
where the time goes in v3:
time: 70.6 us; the launch traced here: 70.3 us
  blocking collectives  53 us (75%)
  Pallas kernels  11.7 us (17%)
  starting transfers between devices  4.88 us (7%)
  between operations  0.71 us (1%)
    all_to_all x2, blocking collectives, exchange(): lax.all_to_all(flat, both, 0, 0, tiled=True, axis_index_groups=members)  32.9 us
    all_to_all x1, blocking collectives, per_device(): gathered = lax.all_to_all(partial, 'dp', 0, 0, tiled=True)  10.4 us
    all_to_all x1, blocking collectives, per_device(): lax.all_to_all(copies, both, 0, 0, tiled=True, axis_index_groups=cubes)  9.6 us
    pallas_call x1, Pallas kernels, per_device(): pl.pallas_call(merge_kernel, out_shape=[pltpu.VMEM((ROWS, c), F32) for c...  4.08 us
    ppermute x1, starting transfers between devices, per_device(): theirs = lax.ppermute(mine, 'dp', swap)  4.02 us
    pallas_call x2, Pallas kernels, product(): pl.pallas_call(functools.partial(product_kernel, own), out_shape=jax.Shap...  3.03 us
    pallas_call x1, Pallas kernels, per_device(): pl.pallas_call(functools.partial(finish_kernel, True), out_shape=next_sha...  2.42 us
    pallas_call x1, Pallas kernels, per_device(): pl.pallas_call(functools.partial(finish_kernel, False), out_shape=next_sh...  1.84 us
  transfers between devices with their start and end apart: 2, of which 0 were waited for; matrix products, arithmetic and copies ran while one was open for 0% of the time, Pallas kernels for 6%

profile of v3, /device:TPU:1, one launch (start us, length us, event | category | flops | bytes accessed | tf_op | source)
XLA Modules:
  0.0 70.3 jit_solution(4301864199692254732)
XLA Ops:
  0.6 4.1 %shard_map.160 = (f32[16,28672]{1,0:T(8,128)S(1)}, f32[16,28672]{1,0:T(8,128)S(1)}, f32[16,8192]{1,0:T(8,128)S(1)}, f32[8,16,128]{2,1,0:T(8,128)S(1)}) custom-call(f32[1,16,28672]{2,1,0:T(8,128)} %refs_0_.1, f32[1,16,28672]{2,1,0:T(8,128)} %refs_1_.1, f32[1,16,8192]{2,1,0:T(8,128)} %refs_2_.1, bf16[1,16,28672]{2,1,0:T(8,128)(2,1)} %refs_3_.1, ...), custom_call_target="tpu_custom_call" | custom-call | flops 10000000 | bytes 7340032 | tf_op jit(solution)/shard_map/pallas_call | solution.py:269
  4.7 10.4 %all_to_all.20.gathered = f32[8,16,128]{2,1,0:T(8,128)S(1)} all-to-all(f32[8,16,128]{2,1,0:T(8,128)S(1)} %get-tuple-element.30), channel_id=1, replica_groups=mesh['dp'=8,'tensor'=16] {'dp'}, dimensions={0} | all-to-all | bytes 131072 | tf_op jit(solution)/shard_map/all_to_all | solution.py:281
  15.2 1.5 %shard_map.162 = f32[1032,128]{1,0:T(8,128)S(1)} custom-call(f32[8,16,128]{2,1,0:T(8,128)S(1)} %all_to_all.20.gathered, f32[16,28672]{1,0:T(8,128)S(1)} %get-tuple-element.31.refs_0_.refs_2_, f32[16,28672]{1,0:T(8,128)S(1)} %get-tuple-element.32.refs_1_.refs_3_, f32[16,8192]{1,0:T(8,128)S(1)} %get-tuple-element.33.refs_2_.refs_4_), custom_call_target="tpu_custom_call" | custom-call | flops 10000000 | bytes 5242880 | tf_op jit(solution)/shard_map/pallas_call | solution.py:292
  16.7 0.9 %collective-permute-start = (f32[1032,128]{1,0:T(8,128)S(1)}, f32[1032,128]{1,0:T(8,128)S(1)}, u32[]{:S(2)}, u32[]{:S(2)}) collective-permute-start(f32[1032,128]{1,0:T(8,128)S(1)} %shard_map.162), channel_id=1, source_target_pairs={{0,16},{16,0},{32,48},{48,32},{64,80},{80,64},{96,112},{112,96},{1... | collective-permute-start | bytes 1585160 | tf_op jit(solution)/shard_map/ppermute | solution.py:303
  17.6 1.5 %shard_map.161 = f32[1032,128]{1,0:T(8,128)S(1)} custom-call(f32[8,16,128]{2,1,0:T(8,128)S(1)} %all_to_all.20.gathered, f32[16,28672]{1,0:T(8,128)S(1)} %get-tuple-element.31.refs_0_.refs_2_, f32[16,28672]{1,0:T(8,128)S(1)} %get-tuple-element.32.refs_1_.refs_3_, f32[16,8192]{1,0:T(8,128)S(1)} %get-tuple-element.33.refs_2_.refs_4_), custom_call_target="tpu_custom_call" | custom-call | flops 10000000 | bytes 5242880 | tf_op jit(solution)/shard_map/pallas_call | solution.py:292
  19.1 0.0 collective-permute-done
  19.1 0.1 add.3
  19.2 12.6 %all_to_all.21 = f32[8,1,16512]{2,1,0:T(1,128)S(1)} all-to-all(f32[8,1,16512]{2,1,0:T(1,128)S(1)} %bitcast.10), channel_id=1, replica_groups={{0,1,4,5,32,33,36,37},{2,3,6,7,34,35,38,39},{8,9,12,13,40,41,44,45},{10..., dimensions={0} | all-to-all | bytes 1056768 | tf_op jit(solution)/shard_map/all_to_all | solution.py:289
  31.8 0.1 shard_map.163
  31.9 20.3 %all_to_all.22 = f32[8,1,16512]{2,1,0:T(1,128)S(1)} all-to-all(f32[8,1,16512]{2,1,0:T(1,128)S(1)} %bitcast.7), channel_id=1, replica_groups={{0,2,8,10,64,66,72,74},{1,3,9,11,65,67,73,75},{4,6,12,14,68,70,76,78},{..., dimensions={0} | all-to-all | bytes 1056768 | tf_op jit(solution)/shard_map/all_to_all | solution.py:289
  52.2 0.3 shard_map.164
  52.4 9.6 %all_to_all.23 = f32[8,128,128]{2,1,0:T(8,128)S(1)} all-to-all(f32[8,128,128]{2,1,0:T(8,128)S(1)} %get-tuple-element.34), channel_id=1, replica_groups={{0,1,4,5,32,33,36,37},{2,3,6,7,34,35,38,39},{8,9,12,13,40,41,44,45},{10..., dimensions={0} | all-to-all | bytes 1048576 | tf_op jit(solution)/shard_map/all_to_all | solution.py:325
  62.0 4.0 %collective-permute-start.1 = (f32[1024,128]{1,0:T(8,128)S(1)}, f32[1024,128]{1,0:T(8,128)S(1)}, u32[]{:S(2)}, u32[]{:S(2)}) collective-permute-start(f32[1024,128]{1,0:T(8,128)S(1)} %bitcast.8), channel_id=1, source_target_pairs={{0,16},{16,0},{32,48},{48,32},{64,80},{80,64},{96,112},{112,96},{1... | collective-permute-start | bytes 1572872 | tf_op jit(solution)/shard_map/ppermute | solution.py:326
  66.1 2.4 %shard_map.165 = (f32[4,28672]{1,0:T(4,128)}, f32[4,28672]{1,0:T(4,128)}, f32[4,8192]{1,0:T(4,128)}, bf16[1,16,28672]{2,1,0:T(8,128)(2,1)}, bf16[1,16,28672]{2,1...) custom-call(f32[1024,128]{1,0:T(8,128)S(1)} %bitcast.9, ...), custom_call_target="tpu_custom_call" | custom-call | flops 10000000 | bytes 4194304 | tf_op jit(solution)/shard_map/pallas_call | solution.py:333
  68.5 0.0 collective-permute-done.1.refs_0_
  68.5 1.8 %shard_map.166 = (f32[4,28672]{1,0:T(4,128)}, f32[4,28672]{1,0:T(4,128)}, f32[4,8192]{1,0:T(4,128)}, bf16[1,16,28672]{2,1,0:T(8,128)(2,1)}, bf16[1,16,28672]{2,1,0:T(8,128)(2,1)}, /*index=5*/bf16[1,16,8192]{2,1,0:T(8,128)(2,1)}) custom-call(f32[1024,128]{1,0:T(8,128)S(1)} %collective-permute-done, ...), custom_call_target="tpu_custom_call", output_to_operand_aliasing={{0}: (5, {}), {1}: (6, {}), {2}: (7, {}), {3}: (8, {}), {4}... | custom-call | flops 10000000 | bytes 4194304 | tf_op jit(solution)/shard_map/pallas_call | solution.py:343
Async XLA Ops:
  16.7 2.4 %collective-permute-start = (f32[1032,128]{1,0:T(8,128)S(1)}, f32[1032,128]{1,0:T(8,128)S(1)}, u32[]{:S(2)}, u32[]{:S(2)}) collective-permute-start(f32[1032,128]{1,0:T(8,128)S(1)} %shard_map.162), channel_id=1, source_target_pairs={{0,16},{16,0},{32,48},{48,32},{64,80},{80,64},{96,112},{112,96},{1... | collective-permute-start | bytes 1585160 | tf_op jit(solution)/shard_map/ppermute | solution.py:303
  62.0 6.5 %collective-permute-start.1 = (f32[1024,128]{1,0:T(8,128)S(1)}, f32[1024,128]{1,0:T(8,128)S(1)}, u32[]{:S(2)}, u32[]{:S(2)}) collective-permute-start(f32[1024,128]{1,0:T(8,128)S(1)} %bitcast.8), channel_id=1, source_target_pairs={{0,16},{16,0},{32,48},{48,32},{64,80},{80,64},{96,112},{112,96},{1... | collective-permute-start | bytes 1572872 | tf_op jit(solution)/shard_map/ppermute | solution.py:326

commit v4 on v2

--- a/solution.py
+++ b/solution.py
@@ -14,11 +14,13 @@
 LANES = 128
 COLS = (28672, 28672, 8192)
 BLOCK = 4 * LANES
-PIECE = 4096
+OTHER_PIECES = ((0, 2048), (0, 4096), (0, 8192), (1, 14336), (2, 4096))
+OWN_PIECES = ((2, 4096), (0, 14336), (1, 8192), (1, 4096), (1, 2048))
 CHIPS = 64
 BLOCK_ROWS = 17
 HALF_BLOCKS = tuple(c // 2 // BLOCK for c in COLS)
 FIRST_BLOCK = (0, HALF_BLOCKS[0], HALF_BLOCKS[0] + HALF_BLOCKS[1])
+HALF = sum(COLS) // 2
 
 
 def lane_iota(rows):
@@ -27,43 +29,47 @@
 
 def merge_kernel(*refs):
     grads, errors, rights = refs[0:3], refs[3:6], refs[6:9]
-    merged, partial = refs[9:12], refs[12]
-    gbuf, ebuf, rbuf, sems = refs[13:16], refs[16:19], refs[19:22], refs[22]
-    copies = []
-    index = 0
-    for m in range(3):
-        for piece in range(COLS[m] // PIECE):
-            cols = pl.ds(piece * PIECE, PIECE)
-            group = [
-                pltpu.make_async_copy(grads[m].at[0, :, cols], gbuf[m].at[:, cols], sems.at[index, 0]),
-                pltpu.make_async_copy(errors[m].at[0, :, cols], ebuf[m].at[:, cols], sems.at[index, 1]),
-            ]
-            if piece == 0:
+    merged, sent, partial = refs[9:12], refs[12], refs[13]
+    gbuf, ebuf, rbuf, sems = refs[14:17], refs[17:20], refs[20:23], refs[23]
+    core = lax.rem(lax.axis_index("dp"), 2)
+    copies, begun = [], set()
+    for own, pieces in ((False, OTHER_PIECES), (True, OWN_PIECES)):
+        done = [0, 0, 0]
+        for m, size in pieces:
+            half = core if own else 1 - core
+            start = pl.multiple_of(half * (COLS[m] // 2) + done[m], LANES)
+            cols = pl.ds(start, size)
+            index = len(copies)
+            group = []
+            if m not in begun:
+                begun.add(m)
                 group.append(pltpu.make_async_copy(rights[m], rbuf[m], sems.at[index, 2]))
+            group.append(pltpu.make_async_copy(grads[m].at[0, :, cols], gbuf[m].at[:, cols], sems.at[index, 0]))
+            group.append(pltpu.make_async_copy(errors[m].at[0, :, cols], ebuf[m].at[:, cols], sems.at[index, 1]))
             for copy in group:
                 copy.start()
-            copies.append((m, piece, group))
-            index += 1
+            copies.append((own, m, start, FIRST_BLOCK[m] * BLOCK + done[m], size, group))
+            done[m] += size
+    totals = [tuple(jnp.zeros((ROWS, LANES), F32) for _ in range(RANK)) for _ in range(3)]
+    for own, m, start, place, size, group in copies:
+        for copy in group:
+            copy.wait()
+
+        def step(j, acc, own=own, m=m, start=start, place=place):
+            cols = pl.ds(pl.multiple_of(start + j * LANES, LANES), LANES)
+            value = gbuf[m][:, cols] + ebuf[m][:, cols].astype(F32)
+            merged[m][:, cols] = value
+            if not own:
+                sent[:, pl.ds(pl.multiple_of(place + j * LANES, LANES), LANES)] = value
+            return tuple(acc[i] + value * rbuf[m][i : i + 1, cols] for i in range(RANK))
+
+        totals[m] = lax.fori_loop(0, size // LANES, step, totals[m], unroll=16)
     lanes = lane_iota(ROWS)
     result = jnp.zeros((ROWS, LANES), F32)
-    totals = None
-    for m, piece, group in copies:
-        if piece == 0:
-            totals = tuple(jnp.zeros((ROWS, LANES), F32) for _ in range(RANK))
-        for copy in group:
-            copy.wait()
-
-        def step(j, acc, m=m, piece=piece):
-            cols = pl.ds(pl.multiple_of(piece * PIECE + j * LANES, LANES), LANES)
-            value = gbuf[m][:, cols] + ebuf[m][:, cols].astype(F32)
-            merged[m][:, cols] = value
-            return tuple(acc[i] + value * rbuf[m][i : i + 1, cols] for i in range(RANK))
-
-        totals = lax.fori_loop(0, PIECE // LANES, step, totals, unroll=8)
-        if piece == COLS[m] // PIECE - 1:
-            for i in range(RANK):
-                column = jnp.sum(totals[i], axis=1, keepdims=True)
-                result = jnp.where(lanes == m * RANK + i, column, result)
+    for m in range(3):
+        for i in range(RANK):
+            column = jnp.sum(totals[m][i], axis=1, keepdims=True)
+            result = jnp.where(lanes == m * RANK + i, column, result)
     for k in range(8):
         partial[k] = result
 
@@ -80,10 +86,9 @@
     return jnp.where(mask, a, b) + pltpu.roll(jnp.where(mask, b, a), 8 - distance, 0)
 
 
-def product_kernel(own, gathered, *refs):
+def product_kernel(gathered, received, *refs):
     merged, out = refs[0:3], refs[3]
     core = lax.rem(lax.axis_index("dp"), 2)
-    half = core if own else 1 - core
     left = sum_replicas(gathered)
     lanes = lane_iota(1)
     gram = jnp.zeros((1, LANES), F32)
@@ -97,13 +102,15 @@
         ]
 
         def step(block, carry, m=m, columns=columns):
-            first = half * (COLS[m] // 2) + block * BLOCK
+            first = core * (COLS[m] // 2) + block * BLOCK
+            place = (FIRST_BLOCK[m] + block) * BLOCK
             row = (FIRST_BLOCK[m] + block) * BLOCK_ROWS
             for pair in range(2):
                 terms = []
                 for b in range(2):
-                    cols = pl.ds(pl.multiple_of(first + (2 * pair + b) * LANES, LANES), LANES)
-                    value = merged[m][:, cols]
+                    shift = (2 * pair + b) * LANES
+                    mine = merged[m][:, pl.ds(pl.multiple_of(first + shift, LANES), LANES)]
+                    value = mine + received[:, pl.ds(pl.multiple_of(place + shift, LANES), LANES)]
                     for i in range(RANK):
                         product = columns[i] * value
                         terms.append(product[:8] + product[8:])
@@ -113,7 +120,7 @@
             out[pl.ds(row + 16, 1), :] = gram
             return carry
 
-        lax.fori_loop(0, HALF_BLOCKS[m], step, 0, unroll=2)
+        lax.fori_loop(0, HALF_BLOCKS[m], step, 0, unroll=4)
 
 
 def solve_kernel(blocks, gathered, copies, left_out, scratch):
@@ -123,7 +130,7 @@
         total[k % 4] = total[k % 4] + blocks[k * BLOCK_ROWS : k * BLOCK_ROWS + 16, :]
         grams[k % 4] = grams[k % 4] + blocks[k * BLOCK_ROWS + 16 : k * BLOCK_ROWS + 17, :]
     scratch[...] = (total[0] + total[1]) + (total[2] + total[3])
-    gram = ((grams[0] + grams[1]) + (grams[2] + grams[3])) * 0.125
+    gram = ((grams[0] + grams[1]) + (grams[2] + grams[3])) * 0.25
 
     def entry(i, j):
         shift = 16 * (i - j) + j
@@ -236,38 +243,35 @@
 
 def per_device(*args):
     grads, errors, rights = args[0:3], args[3:6], args[6:9]
-    pieces = sum(COLS) // PIECE
-    grads, errors, rights = ([pltpu.with_memory_space_constraint(x, pltpu.HBM) for x in group] for group in (grads, errors, rights))
-    *merged, partial = pl.pallas_call(
+    grads, errors, rights = (
+        [pltpu.with_memory_space_constraint(x, pltpu.HBM) for x in group] for group in (grads, errors, rights)
+    )
+    *merged, sent, partial = pl.pallas_call(
         merge_kernel,
-        out_shape=[pltpu.VMEM((ROWS, c), F32) for c in COLS] + [jax.ShapeDtypeStruct((8, ROWS, LANES), F32)],
+        out_shape=[pltpu.VMEM((ROWS, c), F32) for c in COLS]
+        + [jax.ShapeDtypeStruct((ROWS, HALF), F32), jax.ShapeDtypeStruct((8, ROWS, LANES), F32)],
         in_specs=[pl.BlockSpec(memory_space=pltpu.HBM)] * 9,
-        out_specs=[VMEM] * 4,
+        out_specs=[VMEM] * 5,
         scratch_shapes=[pltpu.VMEM((ROWS, c), F32) for c in COLS]
         + [pltpu.VMEM((ROWS, c), BF16) for c in COLS]
         + [pltpu.VMEM((RANK, c), F32) for c in COLS]
-        + [pltpu.SemaphoreType.DMA((pieces, 3))],
+        + [pltpu.SemaphoreType.DMA((len(OTHER_PIECES + OWN_PIECES), 3))],
         compiler_params=PARAMS,
         cost_estimate=cost(10**7, 7 * 2**20),
     )(*grads, *errors, *rights)
+    swap = [(i, i ^ 1) for i in range(8)]
+    received = lax.ppermute(sent, "dp", swap)
     gathered = lax.all_to_all(partial, "dp", 0, 0, tiled=True)
 
     rows = CHIPS * BLOCK_ROWS
-
-    def product(own):
-        return pl.pallas_call(
-            functools.partial(product_kernel, own),
-            out_shape=jax.ShapeDtypeStruct((rows, LANES), F32),
-            in_specs=[VMEM] * 4,
-            out_specs=VMEM,
-            compiler_params=PARAMS,
-            cost_estimate=cost(10**7, 5 * 2**20),
-        )(gathered, *merged)
-
-    swap = [(i, i ^ 1) for i in range(8)]
-    sent = product(False)
-    received = lax.ppermute(sent, "dp", swap)
-    chip_sum = product(True) + received
+    chip_sum = pl.pallas_call(
+        product_kernel,
+        out_shape=jax.ShapeDtypeStruct((rows, LANES), F32),
+        in_specs=[VMEM] * 5,
+        out_specs=VMEM,
+        compiler_params=PARAMS,
+        cost_estimate=cost(10**7, 5 * 2**20),
+    )(gathered, received, *merged)
     both = ("dp", "tensor")
     chips = [[(2 * x + core) * 16 + t for x in range(4) for t in range(16)] for core in range(2)]
     blocks = lax.all_to_all(

time: 64.2 us -> 61.4 us (0.956)
  Pallas kernels: 11.5 us -> 9.79 us
  blocking collectives: 47.4 us -> 45.7 us
  starting transfers between devices: 4.16 us -> 5.01 us
    pallas_call x2 -> x1, Pallas kernels: 2.9 us -> 1.4 us  [per_device(): pl.pallas_call(product_kernel, out_shape=jax.ShapeDtypeStruct((rows, LANE...]
    all_to_all x1, blocking collectives: 10.4 us -> 9.13 us  [per_device(): gathered = lax.all_to_all(partial, 'dp', 0, 0, tiled=True)]
    ppermute x1, starting transfers between devices: 0.86 us -> 1.5 us  [per_device(): received = lax.ppermute(sent, 'dp', swap)]
  transfers between devices with their start and end apart: 2 -> 2, of which waited for: 1 -> 0; matrix products, arithmetic and copies ran while one was open for 0% -> 0% of each run, Pallas kernels for 6% -> 4%
where the time goes in v4:
time: 61.4 us; the launch traced here: 61.2 us
  blocking collectives  45.7 us (74%)
  Pallas kernels  9.79 us (16%)
  starting transfers between devices  5.01 us (8%)
  between operations  0.69 us (1%)
    all_to_all x1, blocking collectives, per_device(): lax.all_to_all(chip_sum.reshape(CHIPS, 1, BLOCK_ROWS * LANES), both, 0, 0...  20.8 us
    all_to_all x1, blocking collectives, per_device(): lax.all_to_all(copies, both, 0, 0, tiled=True, axis_index_groups=chips)  15.7 us
    all_to_all x1, blocking collectives, per_device(): gathered = lax.all_to_all(partial, 'dp', 0, 0, tiled=True)  9.13 us
    pallas_call x1, Pallas kernels, per_device(): pl.pallas_call(merge_kernel, out_shape=[pltpu.VMEM((ROWS, c), F32) for c...  3.86 us
    ppermute x1, starting transfers between devices, per_device(): theirs = lax.ppermute(mine, 'dp', swap)  3.5 us
    pallas_call x1, Pallas kernels, per_device(): pl.pallas_call(functools.partial(finish_kernel, True), out_shape=next_sha...  2.41 us
    pallas_call x1, Pallas kernels, per_device(): pl.pallas_call(functools.partial(finish_kernel, False), out_shape=next_sh...  1.84 us
    ppermute x1, starting transfers between devices, per_device(): received = lax.ppermute(sent, 'dp', swap)  1.5 us
  transfers between devices with their start and end apart: 2, of which 0 were waited for; matrix products, arithmetic and copies ran while one was open for 0% of the time, Pallas kernels for 4%

profile of v4, /device:TPU:1, one launch (start us, length us, event | category | flops | bytes accessed | tf_op | source)
XLA Modules:
  0.0 61.2 jit_solution(719855356013568924)
XLA Ops:
  0.6 3.9 %shard_map.160 = (f32[16,28672]{1,0:T(8,128)S(1)}, f32[16,28672]{1,0:T(8,128)S(1)}, f32[16,8192]{1,0:T(8,128)S(1)}, f32[16,32768]{1,0:T(8,128)S(1)}, f32[8,16,128]{2,1,0:T(8,128)S(1)}) custom-call(f32[1,16,28672]{2,1,0:T(8,128)} %refs_0_.1, f32[1,16,28672]{2,1,0:T(8,128)} %refs_1_.1, f32[1,16,8192]{2,1,0:T(8,128)} %refs_2_.1, bf16[1,16,28672]{2,1,0:T(8,128)(2,1)} %refs_3_.1, ...), custom_call_target="tpu_custom_call" | custom-call | flops 10000000 | bytes 7340032 | tf_op jit(solution)/shard_map/pallas_call | solution.py:249
  4.5 1.5 %collective-permute-start = (f32[16,32768]{1,0:T(8,128)S(1)}, f32[16,32768]{1,0:T(8,128)S(1)}, u32[]{:S(2)}, u32[]{:S(2)}) collective-permute-start(f32[16,32768]{1,0:T(8,128)S(1)} %get-tuple-element.32), channel_id=1, source_target_pairs={{0,16},{16,0},{32,48},{48,32},{64,80},{80,64},{96,112},{112,96},{1... | collective-permute-start | bytes 6291464 | tf_op jit(solution)/shard_map/ppermute | solution.py:263
  6.0 9.1 %all_to_all.15.gathered = f32[8,16,128]{2,1,0:T(8,128)S(1)} all-to-all(f32[8,16,128]{2,1,0:T(8,128)S(1)} %get-tuple-element.31), channel_id=1, replica_groups=mesh['dp'=8,'tensor'=16] {'dp'}, dimensions={0} | all-to-all | bytes 131072 | tf_op jit(solution)/shard_map/all_to_all | solution.py:264
  15.1 0.0 collective-permute-done.received
  15.1 1.4 %shard_map.161 = f32[1088,128]{1,0:T(8,128)S(1)} custom-call(f32[8,16,128]{2,1,0:T(8,128)S(1)} %all_to_all.15.gathered, f32[16,32768]{1,0:T(8,128)S(1)} %collective-permute-done.received, f32[16,28672]{1,0:T(8,128)S(1)} %get-tuple-element.33.refs_0_.refs_2_, f32[16,28672]{1,0:T(8,128)S(1)} %get-tuple-element.34.refs_1_.refs_3_, ...), custom_call_target="tpu_custom_call" | custom-call | flops 10000000 | bytes 5242880 | tf_op jit(solution)/shard_map/pallas_call | solution.py:267
  16.6 20.8 %all_to_all.16 = f32[64,1,2176]{2,1,0:T(1,128)S(1)} all-to-all(f32[64,1,2176]{2,1,0:T(1,128)S(1)} %bitcast.4), channel_id=1, replica_groups={{0,1,2,3,4,5,6,7,8,9,10,11,12,13,14,15,32,33,34,35,36,37,38,39,40,41,42..., dimensions={0} | all-to-all | bytes 1114112 | tf_op jit(solution)/shard_map/all_to_all | solution.py:277
  37.4 0.3 shard_map.162
  37.7 15.7 %all_to_all.17 = f32[64,16,128]{2,1,0:T(8,128)S(1)} all-to-all(f32[64,16,128]{2,1,0:T(8,128)S(1)} %get-tuple-element.36), channel_id=1, replica_groups={{0,1,2,3,4,5,6,7,8,9,10,11,12,13,14,15,32,33,34,35,36,37,38,39,40,41,42..., dimensions={0} | all-to-all | bytes 1048576 | tf_op jit(solution)/shard_map/all_to_all | solution.py:293
  53.4 3.5 %collective-permute-start.1 = (f32[1024,128]{1,0:T(8,128)S(1)}, f32[1024,128]{1,0:T(8,128)S(1)}, u32[]{:S(2)}, u32[]{:S(2)}) collective-permute-start(f32[1024,128]{1,0:T(8,128)S(1)} %bitcast.5), channel_id=1, source_target_pairs={{0,16},{16,0},{32,48},{48,32},{64,80},{80,64},{96,112},{112,96},{1... | collective-permute-start | bytes 1572872 | tf_op jit(solution)/shard_map/ppermute | solution.py:294
  56.9 2.4 %shard_map.163 = (f32[4,28672]{1,0:T(4,128)}, f32[4,28672]{1,0:T(4,128)}, f32[4,8192]{1,0:T(4,128)}, bf16[1,16,28672]{2,1,0:T(8,128)(2,1)}, bf16[1,16,28672]{2,1...) custom-call(f32[1024,128]{1,0:T(8,128)S(1)} %bitcast.6, ...), custom_call_target="tpu_custom_call" | custom-call | flops 10000000 | bytes 4194304 | tf_op jit(solution)/shard_map/pallas_call | solution.py:301
  59.3 0.0 collective-permute-done.1.refs_0_
  59.3 1.8 %shard_map.164 = (f32[4,28672]{1,0:T(4,128)}, f32[4,28672]{1,0:T(4,128)}, f32[4,8192]{1,0:T(4,128)}, bf16[1,16,28672]{2,1,0:T(8,128)(2,1)}, bf16[1,16,28672]{2,1,0:T(8,128)(2,1)}, /*index=5*/bf16[1,16,8192]{2,1,0:T(8,128)(2,1)}) custom-call(f32[1024,128]{1,0:T(8,128)S(1)} %collective-permute-done, ...), custom_call_target="tpu_custom_call", output_to_operand_aliasing={{0}: (5, {}), {1}: (6, {}), {2}: (7, {}), {3}: (8, {}), {4}... | custom-call | flops 10000000 | bytes 4194304 | tf_op jit(solution)/shard_map/pallas_call | solution.py:311
Async XLA Ops:
  4.5 10.6 %collective-permute-start = (f32[16,32768]{1,0:T(8,128)S(1)}, f32[16,32768]{1,0:T(8,128)S(1)}, u32[]{:S(2)}, u32[]{:S(2)}) collective-permute-start(f32[16,32768]{1,0:T(8,128)S(1)} %get-tuple-element.32), channel_id=1, source_target_pairs={{0,16},{16,0},{32,48},{48,32},{64,80},{80,64},{96,112},{112,96},{1... | collective-permute-start | bytes 6291464 | tf_op jit(solution)/shard_map/ppermute | solution.py:263
  53.4 5.9 %collective-permute-start.1 = (f32[1024,128]{1,0:T(8,128)S(1)}, f32[1024,128]{1,0:T(8,128)S(1)}, u32[]{:S(2)}, u32[]{:S(2)}) collective-permute-start(f32[1024,128]{1,0:T(8,128)S(1)} %bitcast.5), channel_id=1, source_target_pairs={{0,16},{16,0},{32,48},{48,32},{64,80},{80,64},{96,112},{112,96},{1... | collective-permute-start | bytes 1572872 | tf_op jit(solution)/shard_map/ppermute | solution.py:294

commit v5 on v4

--- a/solution.py
+++ b/solution.py
@@ -14,8 +14,8 @@
 LANES = 128
 COLS = (28672, 28672, 8192)
 BLOCK = 4 * LANES
-OTHER_PIECES = ((0, 2048), (0, 4096), (0, 8192), (1, 14336), (2, 4096))
-OWN_PIECES = ((2, 4096), (0, 14336), (1, 8192), (1, 4096), (1, 2048))
+OTHER_PIECES = ((0, 4096), (0, 10240), (1, 14336), (2, 4096))
+OWN_PIECES = ((0, 14336), (2, 4096), (1, 10240), (1, 4096))
 CHIPS = 64
 BLOCK_ROWS = 17
 HALF_BLOCKS = tuple(c // 2 // BLOCK for c in COLS)
@@ -32,7 +32,7 @@
     merged, sent, partial = refs[9:12], refs[12], refs[13]
     gbuf, ebuf, rbuf, sems = refs[14:17], refs[17:20], refs[20:23], refs[23]
     core = lax.rem(lax.axis_index("dp"), 2)
-    copies, begun = [], set()
+    copies = []
     for own, pieces in ((False, OTHER_PIECES), (True, OWN_PIECES)):
         done = [0, 0, 0]
         for m, size in pieces:
@@ -41,9 +41,9 @@
             cols = pl.ds(start, size)
             index = len(copies)
             group = []
-            if m not in begun:
-                begun.add(m)
-                group.append(pltpu.make_async_copy(rights[m], rbuf[m], sems.at[index, 2]))
+            if done[m] == 0:
+                whole = pl.ds(start, COLS[m] // 2)
+                group.append(pltpu.make_async_copy(rights[m].at[:, whole], rbuf[m].at[:, whole], sems.at[index, 2]))
             group.append(pltpu.make_async_copy(grads[m].at[0, :, cols], gbuf[m].at[:, cols], sems.at[index, 0]))
             group.append(pltpu.make_async_copy(errors[m].at[0, :, cols], ebuf[m].at[:, cols], sems.at[index, 1]))
             for copy in group:
@@ -70,15 +70,11 @@
         for i in range(RANK):
             column = jnp.sum(totals[m][i], axis=1, keepdims=True)
             result = jnp.where(lanes == m * RANK + i, column, result)
-    for k in range(8):
-        partial[k] = result
-
-
-def sum_replicas(gathered):
-    return (
-        ((gathered[0] + gathered[1]) + (gathered[2] + gathered[3]))
-        + ((gathered[4] + gathered[5]) + (gathered[6] + gathered[7]))
-    ) * 0.125
+    partial[...] = result
+
+
+def sum_replicas(parts):
+    return ((parts[0][...] + parts[2][...]) + (parts[1][...] + parts[3][...])) * 0.125
 
 
 def fold(a, b, distance):
@@ -86,8 +82,8 @@
     return jnp.where(mask, a, b) + pltpu.roll(jnp.where(mask, b, a), 8 - distance, 0)
 
 
-def product_kernel(gathered, received, *refs):
-    merged, out = refs[0:3], refs[3]
+def product_kernel(*refs):
+    gathered, received, merged, out = refs[0:4], refs[4], refs[5:8], refs[8]
     core = lax.rem(lax.axis_index("dp"), 2)
     left = sum_replicas(gathered)
     lanes = lane_iota(1)
@@ -123,7 +119,8 @@
         lax.fori_loop(0, HALF_BLOCKS[m], step, 0, unroll=4)
 
 
-def solve_kernel(blocks, gathered, copies, left_out, scratch):
+def solve_kernel(blocks, *refs):
+    gathered, copies, left_out, scratch = refs[0:4], refs[4], refs[5], refs[6]
     total = [jnp.zeros((16, LANES), F32) for _ in range(4)]
     grams = [jnp.zeros((1, LANES), F32) for _ in range(4)]
     for k in range(CHIPS):
@@ -157,7 +154,7 @@
         left = left + (kept if i == 0 else pltpu.roll(kept, i, 1))
     left_out[...] = left
 
-    mine = (lax.axis_index("dp") // 2) * 16 + lax.axis_index("tensor")
+    mine = CHIPS - 1 - ((lax.axis_index("dp") // 2) * 16 + lax.axis_index("tensor"))
     matrix = jnp.where(mine < FIRST_BLOCK[1], 0, jnp.where(mine < FIRST_BLOCK[2], 1, 2))
     one_lane = lane_iota(1) == matrix * RANK
     nexts = []
@@ -172,27 +169,33 @@
         scratch[pl.ds(i, 4, stride=4), :] = nexts[i]
     block = scratch[...]
     for k in range(CHIPS):
-        copies[k] = block
+        copies[16 * k : 16 * k + 16, :] = block
 
 
 OUT_PIECES = (4, 4, 1)
 
 
 def finish_kernel(own, *refs):
+    rows, left_ref, merged = refs[0], refs[1], refs[2:5]
     if own:
-        rows, left_ref = refs[0:2]
-        merged = refs[2:5]
         nexts, errors, lefts = refs[5:8], refs[8:11], refs[11:14]
-        nbuf, ebuf, square, sems = refs[14:17], refs[17:20], refs[20], refs[21]
+        nbuf, ebuf, sems, square, lbuf, lsems = refs[14:17], refs[17:20], refs[20], refs[21], refs[22:25], refs[25]
     else:
-        rows, left_ref = refs[0:2]
-        merged = refs[2:5]
         nexts, errors = refs[11:14], refs[14:17]
         nbuf, ebuf, sems = refs[17:20], refs[20:23], refs[23]
     core = lax.rem(lax.axis_index("dp"), 2)
     half = core if own else 1 - core
     left = left_ref[...]
     copies = []
+    if own:
+        square[...] = jnp.zeros((LANES, LANES), F32)
+        square[0:ROWS, :] = left
+        turned = square[...].T
+        for m in range(3):
+            lbuf[m][...] = turned[m * RANK : (m + 1) * RANK, 0:ROWS]
+            copy = pltpu.make_async_copy(lbuf[m], lefts[m], lsems.at[m])
+            copy.start()
+            copies.append(copy)
     index = 0
     for m in range(3):
         size = COLS[m] // 2 // OUT_PIECES[m]
@@ -222,12 +225,6 @@
                 copy.start()
                 copies.append(copy)
             index += 1
-    if own:
-        square[...] = jnp.zeros((LANES, LANES), F32)
-        square[0:ROWS, :] = left
-        turned = square[...].T
-        for m in range(3):
-            lefts[m][...] = turned[m * RANK : (m + 1) * RANK, 0:ROWS]
     for copy in copies:
         copy.wait()
 
@@ -249,7 +246,7 @@
     *merged, sent, partial = pl.pallas_call(
         merge_kernel,
         out_shape=[pltpu.VMEM((ROWS, c), F32) for c in COLS]
-        + [jax.ShapeDtypeStruct((ROWS, HALF), F32), jax.ShapeDtypeStruct((8, ROWS, LANES), F32)],
+        + [jax.ShapeDtypeStruct((ROWS, HALF), F32), jax.ShapeDtypeStruct((ROWS, LANES), F32)],
         in_specs=[pl.BlockSpec(memory_space=pltpu.HBM)] * 9,
         out_specs=[VMEM] * 5,
         scratch_shapes=[pltpu.VMEM((ROWS, c), F32) for c in COLS]
@@ -260,20 +257,24 @@
         cost_estimate=cost(10**7, 7 * 2**20),
     )(*grads, *errors, *rights)
     swap = [(i, i ^ 1) for i in range(8)]
+    chip_partial = partial + lax.ppermute(partial, "dp", swap)
+    sent, chip_partial = lax.optimization_barrier((sent, chip_partial))
     received = lax.ppermute(sent, "dp", swap)
-    gathered = lax.all_to_all(partial, "dp", 0, 0, tiled=True)
+    gathered = [chip_partial] + [
+        lax.ppermute(chip_partial, "dp", [(i, (i + 2 * k) % 8) for i in range(8)]) for k in range(1, 4)
+    ]
 
     rows = CHIPS * BLOCK_ROWS
     chip_sum = pl.pallas_call(
         product_kernel,
         out_shape=jax.ShapeDtypeStruct((rows, LANES), F32),
-        in_specs=[VMEM] * 5,
+        in_specs=[VMEM] * 8,
         out_specs=VMEM,
         compiler_params=PARAMS,
         cost_estimate=cost(10**7, 5 * 2**20),
-    )(gathered, received, *merged)
+    )(*gathered, received, *merged)
     both = ("dp", "tensor")
-    chips = [[(2 * x + core) * 16 + t for x in range(4) for t in range(16)] for core in range(2)]
+    chips = [[(2 * x + core) * 16 + t for x in range(3, -1, -1) for t in range(15, -1, -1)] for core in range(2)]
     blocks = lax.all_to_all(
         chip_sum.reshape(CHIPS, 1, BLOCK_ROWS * LANES), both, 0, 0, tiled=True, axis_index_groups=chips
     ).reshape(rows, LANES)
@@ -281,16 +282,18 @@
     copies, left = pl.pallas_call(
         solve_kernel,
         out_shape=[
-            jax.ShapeDtypeStruct((CHIPS, 16, LANES), F32),
+            jax.ShapeDtypeStruct((CHIPS * 16, LANES), F32),
             jax.ShapeDtypeStruct((ROWS, LANES), F32),
         ],
-        in_specs=[VMEM] * 2,
+        in_specs=[VMEM] * 5,
         out_specs=[VMEM] * 2,
         scratch_shapes=[pltpu.VMEM((16, LANES), F32)],
         compiler_params=PARAMS,
         cost_estimate=cost(10**6, 2**20),
-    )(blocks, gathered)
-    mine = lax.all_to_all(copies, both, 0, 0, tiled=True, axis_index_groups=chips).reshape(CHIPS * 16, LANES)
+    )(blocks, *gathered)
+    mine = lax.all_to_all(
+        copies.reshape(CHIPS, 1, 16 * LANES), both, 0, 0, tiled=True, axis_index_groups=chips
+    ).reshape(CHIPS * 16, LANES)
     theirs = lax.ppermute(mine, "dp", swap)
 
     next_shapes = [jax.ShapeDtypeStruct((RANK, c), F32) for c in COLS]
@@ -302,8 +305,11 @@
         functools.partial(finish_kernel, True),
         out_shape=next_shapes + error_shapes + left_shapes,
         in_specs=[VMEM] * 5,
-        out_specs=[ANY] * 6 + [VMEM] * 3,
-        scratch_shapes=scratch + [pltpu.VMEM((LANES, LANES), F32), sems],
+        out_specs=[ANY] * 9,
+        scratch_shapes=scratch
+        + [sems, pltpu.VMEM((LANES, LANES), F32)]
+        + [pltpu.VMEM((RANK, ROWS), F32)] * 3
+        + [pltpu.SemaphoreType.DMA((3,))],
         compiler_params=PARAMS,
         cost_estimate=cost(10**7, 4 * 2**20),
     )(mine, left, *merged)

time: 61.4 us -> 56.8 us (0.925)
  blocking collectives: 45.7 us -> 34.2 us
  starting transfers between devices: 5.01 us -> 10.2 us
  waiting for transfers between devices: 0.01 us -> 2.43 us
  Pallas kernels: 9.79 us -> 9.16 us
    all_to_all x2 -> x1, blocking collectives: 24.8 us -> 16.3 us  [per_device(): lax.all_to_all(copies.reshape(CHIPS, 1, 16 * LANES), both, 0, 0, tiled=Tr...]
    ppermute x0 -> x4, starting transfers between devices: none -> 6.4 us  [the longest x3 4.9 us: per_device(): lax.ppermute(chip_partial, 'dp', [(i, (i + 2 * k) % 8) for i in range(8)])]
    all_to_all x1, blocking collectives: 20.8 us -> 17.9 us  [per_device(): lax.all_to_all(chip_sum.reshape(CHIPS, 1, BLOCK_ROWS * LANES), both, 0, 0...]
    ppermute x0 -> x4, waiting for transfers between devices: none -> 2.43 us  [the longest x3 1.6 us: per_device(): lax.ppermute(chip_partial, 'dp', [(i, (i + 2 * k) % 8) for i in range(8)])]
    ppermute x1, starting transfers between devices: 1.5 us -> 0.34 us  [per_device(): received = lax.ppermute(sent, 'dp', swap)]
  transfers between devices with their start and end apart: 2 -> 6, of which waited for: 0 -> 3; matrix products, arithmetic and copies ran while one was open for 0% -> 0% of each run, Pallas kernels for 4% -> 3%
where the time goes in v5:
time: 56.8 us; the launch traced here: 56.6 us
  blocking collectives  34.2 us (60%)
  starting transfers between devices  10.2 us (18%)
  Pallas kernels  9.16 us (16%)
  waiting for transfers between devices  2.43 us (4%)
  between operations  0.69 us (1%)
    all_to_all x1, blocking collectives, per_device(): lax.all_to_all(chip_sum.reshape(CHIPS, 1, BLOCK_ROWS * LANES), both, 0, 0...  17.9 us
    all_to_all x1, blocking collectives, per_device(): lax.all_to_all(copies.reshape(CHIPS, 1, 16 * LANES), both, 0, 0, tiled=Tr...  16.3 us
    ppermute x3, starting transfers between devices, per_device(): lax.ppermute(chip_partial, 'dp', [(i, (i + 2 * k) % 8) for i in range(8)])  4.9 us
    pallas_call x1, Pallas kernels, per_device(): pl.pallas_call(merge_kernel, out_shape=[pltpu.VMEM((ROWS, c), F32) for c...  3.76 us
    ppermute x1, starting transfers between devices, per_device(): theirs = lax.ppermute(mine, 'dp', swap)  3.41 us
    pallas_call x1, Pallas kernels, per_device(): pl.pallas_call(functools.partial(finish_kernel, True), out_shape=next_sha...  1.88 us
    pallas_call x1, Pallas kernels, per_device(): pl.pallas_call(functools.partial(finish_kernel, False), out_shape=next_sh...  1.84 us
    ppermute x3, waiting for transfers between devices, per_device(): lax.ppermute(chip_partial, 'dp', [(i, (i + 2 * k) % 8) for i in range(8)])  1.6 us
  transfers between devices with their start and end apart: 6, of which 3 were waited for; matrix products, arithmetic and copies ran while one was open for 0% of the time, Pallas kernels for 3%

profile of v5, /device:TPU:1, one launch (start us, length us, event | category | flops | bytes accessed | tf_op | source)
XLA Modules:
  0.0 56.6 jit_solution(6240754142932589513)
XLA Ops:
  0.6 3.8 %shard_map.160 = (f32[16,28672]{1,0:T(8,128)S(1)}, f32[16,28672]{1,0:T(8,128)S(1)}, f32[16,8192]{1,0:T(8,128)S(1)}, f32[16,32768]{1,0:T(8,128)S(1)}, f32[16,128]{1,0:T(8,128)S(1)}) custom-call(f32[1,16,28672]{2,1,0:T(8,128)} %refs_0_.1, f32[1,16,28672]{2,1,0:T(8,128)} %refs_1_.1, f32[1,16,8192]{2,1,0:T(8,128)} %refs_2_.1, bf16[1,16,28672]{2,1,0:T(8,128)(2,1)} %refs_3_.1, ...), custom_call_target="tpu_custom_call" | custom-call | flops 10000000 | bytes 7340032 | tf_op jit(solution)/shard_map/pallas_call | solution.py:246
  4.4 1.5 %collective-permute-start = (f32[16,128]{1,0:T(8,128)S(1)}, f32[16,128]{1,0:T(8,128)S(1)}, u32[]{:S(2)}, u32[]{:S(2)}) collective-permute-start(f32[16,128]{1,0:T(8,128)S(1)} %get-tuple-element.34), channel_id=1, source_target_pairs={{0,16},{16,0},{32,48},{48,32},{64,80},{80,64},{96,112},{112,96},{1... | collective-permute-start | bytes 24584 | tf_op jit(solution)/shard_map/ppermute | solution.py:260
  5.9 0.8 %collective-permute-done = f32[16,128]{1,0:T(8,128)S(1)} collective-permute-done((f32[16,128]{1,0:T(8,128)S(1)}, f32[16,128]{1,0:T(8,128)S(1)}, u32[]{:S(2)}, u32[]{:S(2)}) %collective-permute-start) | collective-permute-done | bytes 8224 | tf_op jit(solution)/shard_map/ppermute | solution.py:260
  6.7 0.3 collective-permute-start.4
  7.1 1.3 %collective-permute-start.1 = (f32[16,128]{1,0:T(8,128)S(1)}, f32[16,128]{1,0:T(8,128)S(1)}, u32[]{:S(2)}, u32[]{:S(2)}) collective-permute-start(f32[16,128]{1,0:T(8,128)S(1)} %add.3.refs_0_), channel_id=1, source_target_pairs={{0,32},{16,48},{32,64},{48,80},{64,96},{80,112},{96,0},{112,16},{1... | collective-permute-start | bytes 24584 | tf_op jit(solution)/shard_map/ppermute | solution.py:264
  8.4 2.5 %collective-permute-start.2 = (f32[16,128]{1,0:T(8,128)S(1)}, f32[16,128]{1,0:T(8,128)S(1)}, u32[]{:S(2)}, u32[]{:S(2)}) collective-permute-start(f32[16,128]{1,0:T(8,128)S(1)} %add.3.refs_0_), channel_id=1, source_target_pairs={{0,64},{16,80},{32,96},{48,112},{64,0},{80,16},{96,32},{112,48},{1... | collective-permute-start | bytes 24584 | tf_op jit(solution)/shard_map/ppermute | solution.py:264
  10.8 1.2 %collective-permute-start.3 = (f32[16,128]{1,0:T(8,128)S(1)}, f32[16,128]{1,0:T(8,128)S(1)}, u32[]{:S(2)}, u32[]{:S(2)}) collective-permute-start(f32[16,128]{1,0:T(8,128)S(1)} %add.3.refs_0_), channel_id=1, source_target_pairs={{0,96},{16,112},{32,0},{48,16},{64,32},{80,48},{96,64},{112,80},{1... | collective-permute-start | bytes 24584 | tf_op jit(solution)/shard_map/ppermute | solution.py:264
  12.0 0.0 collective-permute-done.1.refs_1_
  12.0 0.4 collective-permute-done.2.refs_2_
  12.4 1.2 %collective-permute-done.3.refs_3_ = f32[16,128]{1,0:T(8,128)S(1)} collective-permute-done((f32[16,128]{1,0:T(8,128)S(1)}, f32[16,128]{1,0:T(8,128)S(1)}, u32[]{:S(2)}, u32[]{:S(2)}) %collective-permute-start.3) | collective-permute-done | bytes 8224 | tf_op jit(solution)/shard_map/ppermute | solution.py:264
  13.6 0.0 collective-permute-done.4.refs_4_
  13.6 1.4 %shard_map.161 = f32[1088,128]{1,0:T(8,128)S(1)} custom-call(f32[16,128]{1,0:T(8,128)S(1)} %add.3.refs_0_, f32[16,128]{1,0:T(8,128)S(1)} %collective-permute-done.1.refs_1_, f32[16,128]{1,0:T(8,128)S(1)} %collective-permute-done.2.refs_2_, f32[16,128]{1,0:T(8,128)S(1)} %collective-permute-done.3.refs_3_, f32[16,32768]{1,0:T(8,128)S(1)} %collective-permute-done.4.refs_4_, ...), custom_call_target="tpu_custom_call" | custom-call | flops 10000000 | bytes 5242880 | tf_op jit(solution)/shard_map/pallas_call | solution.py:268
  15.0 17.9 %all_to_all.10 = f32[64,1,2176]{2,1,0:T(1,128)S(1)} all-to-all(f32[64,1,2176]{2,1,0:T(1,128)S(1)} %bitcast.5), channel_id=1, replica_groups={{111,110,109,108,107,106,105,104,103,102,101,100,99,98,97,96,79,78,77,7..., dimensions={0} | all-to-all | bytes 1114112 | tf_op jit(solution)/shard_map/all_to_all | solution.py:278
  32.9 0.3 shard_map.162
  33.2 16.3 %all_to_all.11 = f32[64,1,2048]{2,1,0:T(1,128)S(1)} all-to-all(f32[64,1,2048]{2,1,0:T(1,128)S(1)} %bitcast.8), channel_id=1, replica_groups={{111,110,109,108,107,106,105,104,103,102,101,100,99,98,97,96,79,78,77,7..., dimensions={0} | all-to-all | bytes 1048576 | tf_op jit(solution)/shard_map/all_to_all | solution.py:294
  49.4 3.4 %collective-permute-start.5 = (f32[1024,128]{1,0:T(8,128)S(1)}, f32[1024,128]{1,0:T(8,128)S(1)}, u32[]{:S(2)}, u32[]{:S(2)}) collective-permute-start(f32[1024,128]{1,0:T(8,128)S(1)} %bitcast.6), channel_id=1, source_target_pairs={{0,16},{16,0},{32,48},{48,32},{64,80},{80,64},{96,112},{112,96},{1... | collective-permute-start | bytes 1572872 | tf_op jit(solution)/shard_map/ppermute | solution.py:297
  52.9 1.9 %shard_map.163 = (f32[4,28672]{1,0:T(4,128)}, f32[4,28672]{1,0:T(4,128)}, f32[4,8192]{1,0:T(4,128)}, bf16[1,16,28672]{2,1,0:T(8,128)(2,1)}, bf16[1,16,28672]{2,1...) custom-call(f32[1024,128]{1,0:T(8,128)S(1)} %bitcast.7, ...), custom_call_target="tpu_custom_call" | custom-call | flops 10000000 | bytes 4194304 | tf_op jit(solution)/shard_map/pallas_call | solution.py:304
  54.7 0.0 collective-permute-done.5.refs_0_
  54.8 1.8 %shard_map.164 = (f32[4,28672]{1,0:T(4,128)}, f32[4,28672]{1,0:T(4,128)}, f32[4,8192]{1,0:T(4,128)}, bf16[1,16,28672]{2,1,0:T(8,128)(2,1)}, bf16[1,16,28672]{2,1,0:T(8,128)(2,1)}, /*index=5*/bf16[1,16,8192]{2,1,0:T(8,128)(2,1)}) custom-call(f32[1024,128]{1,0:T(8,128)S(1)} %collective-permute-done, ...), custom_call_target="tpu_custom_call", output_to_operand_aliasing={{0}: (5, {}), {1}: (6, {}), {2}: (7, {}), {3}: (8, {}), {4}... | custom-call | flops 10000000 | bytes 4194304 | tf_op jit(solution)/shard_map/pallas_call | solution.py:317
  (1 shorter events, 0.0 us)
Async XLA Ops:
  4.4 2.3 %collective-permute-start = (f32[16,128]{1,0:T(8,128)S(1)}, f32[16,128]{1,0:T(8,128)S(1)}, u32[]{:S(2)}, u32[]{:S(2)}) collective-permute-start(f32[16,128]{1,0:T(8,128)S(1)} %get-tuple-element.34), channel_id=1, source_target_pairs={{0,16},{16,0},{32,48},{48,32},{64,80},{80,64},{96,112},{112,96},{1... | collective-permute-start | bytes 24584 | tf_op jit(solution)/shard_map/ppermute | solution.py:260
  6.7 6.8 %collective-permute-start.4 = (f32[16,32768]{1,0:T(8,128)S(1)}, f32[16,32768]{1,0:T(8,128)S(1)}, u32[]{:S(2)}, u32[]{:S(2)}) collective-permute-start(f32[16,32768]{1,0:T(8,128)S(1)} %get-tuple-element.36), channel_id=1, source_target_pairs={{0,16},{16,0},{32,48},{48,32},{64,80},{80,64},{96,112},{112,96},{1... | collective-permute-start | bytes 6291464 | tf_op jit(solution)/shard_map/ppermute | solution.py:262
  7.1 4.9 %collective-permute-start.1 = (f32[16,128]{1,0:T(8,128)S(1)}, f32[16,128]{1,0:T(8,128)S(1)}, u32[]{:S(2)}, u32[]{:S(2)}) collective-permute-start(f32[16,128]{1,0:T(8,128)S(1)} %add.3.refs_0_), channel_id=1, source_target_pairs={{0,32},{16,48},{32,64},{48,80},{64,96},{80,112},{96,0},{112,16},{1... | collective-permute-start | bytes 24584 | tf_op jit(solution)/shard_map/ppermute | solution.py:264
  8.4 4.0 %collective-permute-start.2 = (f32[16,128]{1,0:T(8,128)S(1)}, f32[16,128]{1,0:T(8,128)S(1)}, u32[]{:S(2)}, u32[]{:S(2)}) collective-permute-start(f32[16,128]{1,0:T(8,128)S(1)} %add.3.refs_0_), channel_id=1, source_target_pairs={{0,64},{16,80},{32,96},{48,112},{64,0},{80,16},{96,32},{112,48},{1... | collective-permute-start | bytes 24584 | tf_op jit(solution)/shard_map/ppermute | solution.py:264
  10.8 2.8 %collective-permute-start.3 = (f32[16,128]{1,0:T(8,128)S(1)}, f32[16,128]{1,0:T(8,128)S(1)}, u32[]{:S(2)}, u32[]{:S(2)}) collective-permute-start(f32[16,128]{1,0:T(8,128)S(1)} %add.3.refs_0_), channel_id=1, source_target_pairs={{0,96},{16,112},{32,0},{48,16},{64,32},{80,48},{96,64},{112,80},{1... | collective-permute-start | bytes 24584 | tf_op jit(solution)/shard_map/ppermute | solution.py:264
  49.4 5.3 %collective-permute-start.5 = (f32[1024,128]{1,0:T(8,128)S(1)}, f32[1024,128]{1,0:T(8,128)S(1)}, u32[]{:S(2)}, u32[]{:S(2)}) collective-permute-start(f32[1024,128]{1,0:T(8,128)S(1)} %bitcast.6), channel_id=1, source_target_pairs={{0,16},{16,0},{32,48},{48,32},{64,80},{80,64},{96,112},{112,96},{1... | collective-permute-start | bytes 1572872 | tf_op jit(solution)/shard_map/ppermute | solution.py:297

commit v6 on v5

--- a/solution.py
+++ b/solution.py
@@ -154,7 +154,9 @@
         left = left + (kept if i == 0 else pltpu.roll(kept, i, 1))
     left_out[...] = left
 
-    mine = CHIPS - 1 - ((lax.axis_index("dp") // 2) * 16 + lax.axis_index("tensor"))
+    tensor = lax.axis_index("tensor")
+    x, z, y = lax.div(lax.axis_index("dp"), 2), lax.div(tensor, 4), lax.rem(tensor, 4)
+    mine = lax.rem(6 - x, 4) * 16 + lax.rem(6 - z, 4) * 4 + lax.rem(6 - y, 4)
     matrix = jnp.where(mine < FIRST_BLOCK[1], 0, jnp.where(mine < FIRST_BLOCK[2], 1, 2))
     one_lane = lane_iota(1) == matrix * RANK
     nexts = []
@@ -274,7 +276,8 @@
         cost_estimate=cost(10**7, 5 * 2**20),
     )(*gathered, received, *merged)
     both = ("dp", "tensor")
-    chips = [[(2 * x + core) * 16 + t for x in range(3, -1, -1) for t in range(15, -1, -1)] for core in range(2)]
+    down = (2, 1, 0, 3)
+    chips = [[(2 * x + core) * 16 + z * 4 + y for x in down for z in down for y in down] for core in range(2)]
     blocks = lax.all_to_all(
         chip_sum.reshape(CHIPS, 1, BLOCK_ROWS * LANES), both, 0, 0, tiled=True, axis_index_groups=chips
     ).reshape(rows, LANES)

time: 56.8 us -> 55.7 us (0.981)
  blocking collectives: 34.2 us -> 32.4 us
  starting transfers between devices: 10.2 us -> 10.8 us
    all_to_all x1, blocking collectives: 16.3 us -> 14.9 us  [per_device(): lax.all_to_all(copies.reshape(CHIPS, 1, 16 * LANES), both, 0, 0, tiled=Tr...]
    ppermute x1, starting transfers between devices: 3.41 us -> 4.02 us  [per_device(): theirs = lax.ppermute(mine, 'dp', swap)]
where the time goes in v6:
time: 55.7 us; the launch traced here: 55.5 us
  blocking collectives  32.4 us (58%)
  starting transfers between devices  10.8 us (19%)
  Pallas kernels  9.16 us (16%)
  waiting for transfers between devices  2.43 us (4%)
  between operations  0.69 us (1%)
    all_to_all x1, blocking collectives, per_device(): lax.all_to_all(chip_sum.reshape(CHIPS, 1, BLOCK_ROWS * LANES), both, 0, 0...  17.5 us
    all_to_all x1, blocking collectives, per_device(): lax.all_to_all(copies.reshape(CHIPS, 1, 16 * LANES), both, 0, 0, tiled=Tr...  14.9 us
    ppermute x3, starting transfers between devices, per_device(): lax.ppermute(chip_partial, 'dp', [(i, (i + 2 * k) % 8) for i in range(8)])  4.9 us
    ppermute x1, starting transfers between devices, per_device(): theirs = lax.ppermute(mine, 'dp', swap)  4.02 us
    pallas_call x1, Pallas kernels, per_device(): pl.pallas_call(merge_kernel, out_shape=[pltpu.VMEM((ROWS, c), F32) for c...  3.76 us
    pallas_call x1, Pallas kernels, per_device(): pl.pallas_call(functools.partial(finish_kernel, True), out_shape=next_sha...  1.88 us
    pallas_call x1, Pallas kernels, per_device(): pl.pallas_call(functools.partial(finish_kernel, False), out_shape=next_sh...  1.84 us
    ppermute x3, waiting for transfers between devices, per_device(): lax.ppermute(chip_partial, 'dp', [(i, (i + 2 * k) % 8) for i in range(8)])  1.6 us
  transfers between devices with their start and end apart: 6, of which 3 were waited for; matrix products, arithmetic and copies ran while one was open for 0% of the time, Pallas kernels for 3%

profile of v6, /device:TPU:1, one launch (start us, length us, event | category | flops | bytes accessed | tf_op | source)
XLA Modules:
  0.0 55.5 jit_solution(8769721946886139124)
XLA Ops:
  0.6 3.8 %shard_map.160 = (f32[16,28672]{1,0:T(8,128)S(1)}, f32[16,28672]{1,0:T(8,128)S(1)}, f32[16,8192]{1,0:T(8,128)S(1)}, f32[16,32768]{1,0:T(8,128)S(1)}, f32[16,128]{1,0:T(8,128)S(1)}) custom-call(f32[1,16,28672]{2,1,0:T(8,128)} %refs_0_.1, f32[1,16,28672]{2,1,0:T(8,128)} %refs_1_.1, f32[1,16,8192]{2,1,0:T(8,128)} %refs_2_.1, bf16[1,16,28672]{2,1,0:T(8,128)(2,1)} %refs_3_.1, ...), custom_call_target="tpu_custom_call" | custom-call | flops 10000000 | bytes 7340032 | tf_op jit(solution)/shard_map/pallas_call | solution.py:248
  4.4 1.5 %collective-permute-start = (f32[16,128]{1,0:T(8,128)S(1)}, f32[16,128]{1,0:T(8,128)S(1)}, u32[]{:S(2)}, u32[]{:S(2)}) collective-permute-start(f32[16,128]{1,0:T(8,128)S(1)} %get-tuple-element.34), channel_id=1, source_target_pairs={{0,16},{16,0},{32,48},{48,32},{64,80},{80,64},{96,112},{112,96},{1... | collective-permute-start | bytes 24584 | tf_op jit(solution)/shard_map/ppermute | solution.py:262
  5.9 0.8 %collective-permute-done = f32[16,128]{1,0:T(8,128)S(1)} collective-permute-done((f32[16,128]{1,0:T(8,128)S(1)}, f32[16,128]{1,0:T(8,128)S(1)}, u32[]{:S(2)}, u32[]{:S(2)}) %collective-permute-start) | collective-permute-done | bytes 8224 | tf_op jit(solution)/shard_map/ppermute | solution.py:262
  6.7 0.3 collective-permute-start.4
  7.1 1.3 %collective-permute-start.1 = (f32[16,128]{1,0:T(8,128)S(1)}, f32[16,128]{1,0:T(8,128)S(1)}, u32[]{:S(2)}, u32[]{:S(2)}) collective-permute-start(f32[16,128]{1,0:T(8,128)S(1)} %add.3.refs_0_), channel_id=1, source_target_pairs={{0,32},{16,48},{32,64},{48,80},{64,96},{80,112},{96,0},{112,16},{1... | collective-permute-start | bytes 24584 | tf_op jit(solution)/shard_map/ppermute | solution.py:266
  8.4 2.5 %collective-permute-start.2 = (f32[16,128]{1,0:T(8,128)S(1)}, f32[16,128]{1,0:T(8,128)S(1)}, u32[]{:S(2)}, u32[]{:S(2)}) collective-permute-start(f32[16,128]{1,0:T(8,128)S(1)} %add.3.refs_0_), channel_id=1, source_target_pairs={{0,64},{16,80},{32,96},{48,112},{64,0},{80,16},{96,32},{112,48},{1... | collective-permute-start | bytes 24584 | tf_op jit(solution)/shard_map/ppermute | solution.py:266
  10.8 1.2 %collective-permute-start.3 = (f32[16,128]{1,0:T(8,128)S(1)}, f32[16,128]{1,0:T(8,128)S(1)}, u32[]{:S(2)}, u32[]{:S(2)}) collective-permute-start(f32[16,128]{1,0:T(8,128)S(1)} %add.3.refs_0_), channel_id=1, source_target_pairs={{0,96},{16,112},{32,0},{48,16},{64,32},{80,48},{96,64},{112,80},{1... | collective-permute-start | bytes 24584 | tf_op jit(solution)/shard_map/ppermute | solution.py:266
  12.0 0.0 collective-permute-done.1.refs_1_
  12.0 0.4 collective-permute-done.2.refs_2_
  12.4 1.2 %collective-permute-done.3.refs_3_ = f32[16,128]{1,0:T(8,128)S(1)} collective-permute-done((f32[16,128]{1,0:T(8,128)S(1)}, f32[16,128]{1,0:T(8,128)S(1)}, u32[]{:S(2)}, u32[]{:S(2)}) %collective-permute-start.3) | collective-permute-done | bytes 8224 | tf_op jit(solution)/shard_map/ppermute | solution.py:266
  13.6 0.0 collective-permute-done.4.refs_4_
  13.6 1.4 %shard_map.161 = f32[1088,128]{1,0:T(8,128)S(1)} custom-call(f32[16,128]{1,0:T(8,128)S(1)} %add.3.refs_0_, f32[16,128]{1,0:T(8,128)S(1)} %collective-permute-done.1.refs_1_, f32[16,128]{1,0:T(8,128)S(1)} %collective-permute-done.2.refs_2_, f32[16,128]{1,0:T(8,128)S(1)} %collective-permute-done.3.refs_3_, f32[16,32768]{1,0:T(8,128)S(1)} %collective-permute-done.4.refs_4_, ...), custom_call_target="tpu_custom_call" | custom-call | flops 10000000 | bytes 5242880 | tf_op jit(solution)/shard_map/pallas_call | solution.py:270
  15.0 17.5 %all_to_all.10 = f32[64,1,2176]{2,1,0:T(1,128)S(1)} all-to-all(f32[64,1,2176]{2,1,0:T(1,128)S(1)} %bitcast.5), channel_id=1, replica_groups={{74,73,72,75,70,69,68,71,66,65,64,67,78,77,76,79,42,41,40,43,38,37,36,3..., dimensions={0} | all-to-all | bytes 1114112 | tf_op jit(solution)/shard_map/all_to_all | solution.py:281
  32.5 0.3 shard_map.162
  32.8 14.9 %all_to_all.11 = f32[64,1,2048]{2,1,0:T(1,128)S(1)} all-to-all(f32[64,1,2048]{2,1,0:T(1,128)S(1)} %bitcast.8), channel_id=1, replica_groups={{74,73,72,75,70,69,68,71,66,65,64,67,78,77,76,79,42,41,40,43,38,37,36,3..., dimensions={0} | all-to-all | bytes 1048576 | tf_op jit(solution)/shard_map/all_to_all | solution.py:297
  47.7 4.0 %collective-permute-start.5 = (f32[1024,128]{1,0:T(8,128)S(1)}, f32[1024,128]{1,0:T(8,128)S(1)}, u32[]{:S(2)}, u32[]{:S(2)}) collective-permute-start(f32[1024,128]{1,0:T(8,128)S(1)} %bitcast.6), channel_id=1, source_target_pairs={{0,16},{16,0},{32,48},{48,32},{64,80},{80,64},{96,112},{112,96},{1... | collective-permute-start | bytes 1572872 | tf_op jit(solution)/shard_map/ppermute | solution.py:300
  51.7 1.9 %shard_map.163 = (f32[4,28672]{1,0:T(4,128)}, f32[4,28672]{1,0:T(4,128)}, f32[4,8192]{1,0:T(4,128)}, bf16[1,16,28672]{2,1,0:T(8,128)(2,1)}, bf16[1,16,28672]{2,1...) custom-call(f32[1024,128]{1,0:T(8,128)S(1)} %bitcast.7, ...), custom_call_target="tpu_custom_call" | custom-call | flops 10000000 | bytes 4194304 | tf_op jit(solution)/shard_map/pallas_call | solution.py:307
  53.6 0.0 collective-permute-done.5.refs_0_
  53.6 1.8 %shard_map.164 = (f32[4,28672]{1,0:T(4,128)}, f32[4,28672]{1,0:T(4,128)}, f32[4,8192]{1,0:T(4,128)}, bf16[1,16,28672]{2,1,0:T(8,128)(2,1)}, bf16[1,16,28672]{2,1,0:T(8,128)(2,1)}, /*index=5*/bf16[1,16,8192]{2,1,0:T(8,128)(2,1)}) custom-call(f32[1024,128]{1,0:T(8,128)S(1)} %collective-permute-done, ...), custom_call_target="tpu_custom_call", output_to_operand_aliasing={{0}: (5, {}), {1}: (6, {}), {2}: (7, {}), {3}: (8, {}), {4}... | custom-call | flops 10000000 | bytes 4194304 | tf_op jit(solution)/shard_map/pallas_call | solution.py:320
  (1 shorter events, 0.0 us)
Async XLA Ops:
  4.4 2.3 %collective-permute-start = (f32[16,128]{1,0:T(8,128)S(1)}, f32[16,128]{1,0:T(8,128)S(1)}, u32[]{:S(2)}, u32[]{:S(2)}) collective-permute-start(f32[16,128]{1,0:T(8,128)S(1)} %get-tuple-element.34), channel_id=1, source_target_pairs={{0,16},{16,0},{32,48},{48,32},{64,80},{80,64},{96,112},{112,96},{1... | collective-permute-start | bytes 24584 | tf_op jit(solution)/shard_map/ppermute | solution.py:262
  6.7 6.8 %collective-permute-start.4 = (f32[16,32768]{1,0:T(8,128)S(1)}, f32[16,32768]{1,0:T(8,128)S(1)}, u32[]{:S(2)}, u32[]{:S(2)}) collective-permute-start(f32[16,32768]{1,0:T(8,128)S(1)} %get-tuple-element.36), channel_id=1, source_target_pairs={{0,16},{16,0},{32,48},{48,32},{64,80},{80,64},{96,112},{112,96},{1... | collective-permute-start | bytes 6291464 | tf_op jit(solution)/shard_map/ppermute | solution.py:264
  7.1 4.9 %collective-permute-start.1 = (f32[16,128]{1,0:T(8,128)S(1)}, f32[16,128]{1,0:T(8,128)S(1)}, u32[]{:S(2)}, u32[]{:S(2)}) collective-permute-start(f32[16,128]{1,0:T(8,128)S(1)} %add.3.refs_0_), channel_id=1, source_target_pairs={{0,32},{16,48},{32,64},{48,80},{64,96},{80,112},{96,0},{112,16},{1... | collective-permute-start | bytes 24584 | tf_op jit(solution)/shard_map/ppermute | solution.py:266
  8.4 4.0 %collective-permute-start.2 = (f32[16,128]{1,0:T(8,128)S(1)}, f32[16,128]{1,0:T(8,128)S(1)}, u32[]{:S(2)}, u32[]{:S(2)}) collective-permute-start(f32[16,128]{1,0:T(8,128)S(1)} %add.3.refs_0_), channel_id=1, source_target_pairs={{0,64},{16,80},{32,96},{48,112},{64,0},{80,16},{96,32},{112,48},{1... | collective-permute-start | bytes 24584 | tf_op jit(solution)/shard_map/ppermute | solution.py:266
  10.8 2.8 %collective-permute-start.3 = (f32[16,128]{1,0:T(8,128)S(1)}, f32[16,128]{1,0:T(8,128)S(1)}, u32[]{:S(2)}, u32[]{:S(2)}) collective-permute-start(f32[16,128]{1,0:T(8,128)S(1)} %add.3.refs_0_), channel_id=1, source_target_pairs={{0,96},{16,112},{32,0},{48,16},{64,32},{80,48},{96,64},{112,80},{1... | collective-permute-start | bytes 24584 | tf_op jit(solution)/shard_map/ppermute | solution.py:266
  47.7 5.9 %collective-permute-start.5 = (f32[1024,128]{1,0:T(8,128)S(1)}, f32[1024,128]{1,0:T(8,128)S(1)}, u32[]{:S(2)}, u32[]{:S(2)}) collective-permute-start(f32[1024,128]{1,0:T(8,128)S(1)} %bitcast.6), channel_id=1, source_target_pairs={{0,16},{16,0},{32,48},{48,32},{64,80},{80,64},{96,112},{112,96},{1... | collective-permute-start | bytes 1572872 | tf_op jit(solution)/shard_map/ppermute | solution.py:300

commit v7 on v6

--- a/solution.py
+++ b/solution.py
@@ -77,46 +77,55 @@
     return ((parts[0][...] + parts[2][...]) + (parts[1][...] + parts[3][...])) * 0.125
 
 
-def fold(a, b, distance):
-    mask = (lax.broadcasted_iota(jnp.int32, (8, LANES), 0) & distance) == 0
-    return jnp.where(mask, a, b) + pltpu.roll(jnp.where(mask, b, a), 8 - distance, 0)
+def split_kernel(received, *refs):
+    merged, parts = refs[0:3], refs[3]
+    core = lax.rem(lax.axis_index("dp"), 2)
+    for m in range(3):
+
+        def step(j, carry, m=m):
+            here = pl.ds(pl.multiple_of(FIRST_BLOCK[m] * BLOCK + j * LANES, LANES), LANES)
+            mine = merged[m][:, pl.ds(pl.multiple_of(core * (COLS[m] // 2) + j * LANES, LANES), LANES)]
+            value = mine + received[:, here]
+            high = value.astype(BF16)
+            parts[0:ROWS, here] = high
+            parts[ROWS : 2 * ROWS, here] = (value - high.astype(F32)).astype(BF16)
+            return carry
+
+        lax.fori_loop(0, COLS[m] // 2 // LANES, step, 0, unroll=16)
 
 
 def product_kernel(*refs):
-    gathered, received, merged, out = refs[0:4], refs[4], refs[5:8], refs[8]
-    core = lax.rem(lax.axis_index("dp"), 2)
+    gathered, parts, out, square = refs[0:4], refs[4], refs[5], refs[6]
     left = sum_replicas(gathered)
+    square[...] = jnp.zeros((LANES, LANES), F32)
+    square[0:ROWS, :] = left
+    turned = square[...].T[0 : 3 * RANK, 0:ROWS]
+    high = turned.astype(BF16).astype(F32)
+    low = turned - high
+    for m in range(3):
+        mine = slice(m * RANK, (m + 1) * RANK)
+        factors = jnp.concatenate(
+            [
+                jnp.concatenate([high[mine], high[mine]], axis=1),
+                jnp.concatenate([low[mine], low[mine]], axis=1),
+            ],
+            axis=0,
+        ).astype(BF16)
+        start = FIRST_BLOCK[m] * BLOCK
+        both = jnp.dot(factors, parts[:, start : start + COLS[m] // 2], preferred_element_type=F32)
+        for j in range(COLS[m] // 2 // LANES):
+            place = FIRST_BLOCK[m] * 4 + j
+            row = place // 4 * BLOCK_ROWS + place % 4 * RANK
+            value = both[:, j * LANES : (j + 1) * LANES]
+            out[row : row + RANK, :] = value[0:RANK] + value[RANK : 2 * RANK]
     lanes = lane_iota(1)
     gram = jnp.zeros((1, LANES), F32)
     for shift in range(RANK):
         other = left if shift == 0 else pltpu.roll(left, LANES - shift, 1)
         row = jnp.where(lanes < 3 * RANK, jnp.sum(left * other, axis=0, keepdims=True), 0.0)
         gram = gram + (row if shift == 0 else pltpu.roll(row, 16 * shift, 1))
-    for m in range(3):
-        columns = [
-            jnp.broadcast_to(left[:, m * RANK + i : m * RANK + i + 1], (ROWS, LANES)) for i in range(RANK)
-        ]
-
-        def step(block, carry, m=m, columns=columns):
-            first = core * (COLS[m] // 2) + block * BLOCK
-            place = (FIRST_BLOCK[m] + block) * BLOCK
-            row = (FIRST_BLOCK[m] + block) * BLOCK_ROWS
-            for pair in range(2):
-                terms = []
-                for b in range(2):
-                    shift = (2 * pair + b) * LANES
-                    mine = merged[m][:, pl.ds(pl.multiple_of(first + shift, LANES), LANES)]
-                    value = mine + received[:, pl.ds(pl.multiple_of(place + shift, LANES), LANES)]
-                    for i in range(RANK):
-                        product = columns[i] * value
-                        terms.append(product[:8] + product[8:])
-                ones = [fold(terms[2 * k], terms[2 * k + 1], 1) for k in range(4)]
-                twos = [fold(ones[2 * k], ones[2 * k + 1], 2) for k in range(2)]
-                out[pl.ds(row + 8 * pair, 8), :] = fold(twos[0], twos[1], 4)
-            out[pl.ds(row + 16, 1), :] = gram
-            return carry
-
-        lax.fori_loop(0, HALF_BLOCKS[m], step, 0, unroll=4)
+    for k in range(CHIPS):
+        out[k * BLOCK_ROWS + 16 : (k + 1) * BLOCK_ROWS, :] = gram
 
 
 def solve_kernel(blocks, *refs):
@@ -267,14 +276,23 @@
     ]
 
     rows = CHIPS * BLOCK_ROWS
+    parts = pl.pallas_call(
+        split_kernel,
+        out_shape=jax.ShapeDtypeStruct((2 * ROWS, HALF), BF16),
+        in_specs=[VMEM] * 4,
+        out_specs=VMEM,
+        compiler_params=PARAMS,
+        cost_estimate=cost(10**7, 6 * 2**20),
+    )(received, *merged)
     chip_sum = pl.pallas_call(
         product_kernel,
         out_shape=jax.ShapeDtypeStruct((rows, LANES), F32),
-        in_specs=[VMEM] * 8,
+        in_specs=[VMEM] * 5,
         out_specs=VMEM,
-        compiler_params=PARAMS,
-        cost_estimate=cost(10**7, 5 * 2**20),
-    )(*gathered, received, *merged)
+        scratch_shapes=[pltpu.VMEM((LANES, LANES), F32)],
+        compiler_params=PARAMS,
+        cost_estimate=cost(10**7, 3 * 2**20),
+    )(*gathered, parts)
     both = ("dp", "tensor")
     down = (2, 1, 0, 3)
     chips = [[(2 * x + core) * 16 + z * 4 + y for x in down for z in down for y in down] for core in range(2)]

time: 55.7 us -> 54.8 us (0.984)
  waiting for transfers between devices: 2.43 us -> 1.3 us
    ppermute x3, waiting for transfers between devices: 1.6 us -> 0.46 us  [per_device(): lax.ppermute(chip_partial, 'dp', [(i, (i + 2 * k) % 8) for i in range(8)])]
    pallas_call x0 -> x1, Pallas kernels: none -> 1.11 us  [per_device(): pl.pallas_call(split_kernel, out_shape=jax.ShapeDtypeStruct((2 * ROWS, HA...]
    pallas_call x1, Pallas kernels: 1.4 us -> 0.56 us  [per_device(): pl.pallas_call(product_kernel, out_shape=jax.ShapeDtypeStruct((rows, LANE...]
  transfers between devices with their start and end apart: 6 -> 6, of which waited for: 3 -> 2; matrix products, arithmetic and copies ran while one was open for 0% -> 0% of each run, Pallas kernels for 3% -> 5%
where the time goes in v7:
time: 54.8 us; the launch traced here: 54.6 us
  blocking collectives  32.4 us (59%)
  starting transfers between devices  10.8 us (20%)
  Pallas kernels  9.43 us (17%)
  waiting for transfers between devices  1.3 us (2%)
  between operations  0.71 us (1%)
    all_to_all x1, blocking collectives, per_device(): lax.all_to_all(chip_sum.reshape(CHIPS, 1, BLOCK_ROWS * LANES), both, 0, 0...  17.5 us
    all_to_all x1, blocking collectives, per_device(): lax.all_to_all(copies.reshape(CHIPS, 1, 16 * LANES), both, 0, 0, tiled=Tr...  14.9 us
    ppermute x3, starting transfers between devices, per_device(): lax.ppermute(chip_partial, 'dp', [(i, (i + 2 * k) % 8) for i in range(8)])  4.9 us
    ppermute x1, starting transfers between devices, per_device(): theirs = lax.ppermute(mine, 'dp', swap)  4.02 us
    pallas_call x1, Pallas kernels, per_device(): pl.pallas_call(merge_kernel, out_shape=[pltpu.VMEM((ROWS, c), F32) for c...  3.76 us
    pallas_call x1, Pallas kernels, per_device(): pl.pallas_call(functools.partial(finish_kernel, True), out_shape=next_sha...  1.88 us
    pallas_call x1, Pallas kernels, per_device(): pl.pallas_call(functools.partial(finish_kernel, False), out_shape=next_sh...  1.84 us
    ppermute x1, starting transfers between devices, per_device(): chip_partial = partial + lax.ppermute(partial, 'dp', swap)  1.5 us
  transfers between devices with their start and end apart: 6, of which 2 were waited for; matrix products, arithmetic and copies ran while one was open for 0% of the time, Pallas kernels for 5%

profile of v7, /device:TPU:1, one launch (start us, length us, event | category | flops | bytes accessed | tf_op | source)
XLA Modules:
  0.0 54.6 jit_solution(16734423882565401401)
XLA Ops:
  0.6 3.8 %shard_map.160 = (f32[16,28672]{1,0:T(8,128)S(1)}, f32[16,28672]{1,0:T(8,128)S(1)}, f32[16,8192]{1,0:T(8,128)S(1)}, f32[16,32768]{1,0:T(8,128)S(1)}, f32[16,128]{1,0:T(8,128)S(1)}) custom-call(f32[1,16,28672]{2,1,0:T(8,128)} %refs_0_.1, f32[1,16,28672]{2,1,0:T(8,128)} %refs_1_.1, f32[1,16,8192]{2,1,0:T(8,128)} %refs_2_.1, bf16[1,16,28672]{2,1,0:T(8,128)(2,1)} %refs_3_.1, ...), custom_call_target="tpu_custom_call" | custom-call | flops 10000000 | bytes 7340032 | tf_op jit(solution)/shard_map/pallas_call | solution.py:257
  4.4 1.5 %collective-permute-start = (f32[16,128]{1,0:T(8,128)S(1)}, f32[16,128]{1,0:T(8,128)S(1)}, u32[]{:S(2)}, u32[]{:S(2)}) collective-permute-start(f32[16,128]{1,0:T(8,128)S(1)} %get-tuple-element.34), channel_id=1, source_target_pairs={{0,16},{16,0},{32,48},{48,32},{64,80},{80,64},{96,112},{112,96},{1... | collective-permute-start | bytes 24584 | tf_op jit(solution)/shard_map/ppermute | solution.py:271
  5.9 0.8 %collective-permute-done = f32[16,128]{1,0:T(8,128)S(1)} collective-permute-done((f32[16,128]{1,0:T(8,128)S(1)}, f32[16,128]{1,0:T(8,128)S(1)}, u32[]{:S(2)}, u32[]{:S(2)}) %collective-permute-start) | collective-permute-done | bytes 8224 | tf_op jit(solution)/shard_map/ppermute | solution.py:271
  6.7 0.3 collective-permute-start.4
  7.1 1.3 %collective-permute-start.1 = (f32[16,128]{1,0:T(8,128)S(1)}, f32[16,128]{1,0:T(8,128)S(1)}, u32[]{:S(2)}, u32[]{:S(2)}) collective-permute-start(f32[16,128]{1,0:T(8,128)S(1)} %add.3.refs_0_), channel_id=1, source_target_pairs={{0,32},{16,48},{32,64},{48,80},{64,96},{80,112},{96,0},{112,16},{1... | collective-permute-start | bytes 24584 | tf_op jit(solution)/shard_map/ppermute | solution.py:275
  8.4 2.5 %collective-permute-start.2 = (f32[16,128]{1,0:T(8,128)S(1)}, f32[16,128]{1,0:T(8,128)S(1)}, u32[]{:S(2)}, u32[]{:S(2)}) collective-permute-start(f32[16,128]{1,0:T(8,128)S(1)} %add.3.refs_0_), channel_id=1, source_target_pairs={{0,64},{16,80},{32,96},{48,112},{64,0},{80,16},{96,32},{112,48},{1... | collective-permute-start | bytes 24584 | tf_op jit(solution)/shard_map/ppermute | solution.py:275
  10.8 1.2 %collective-permute-start.3 = (f32[16,128]{1,0:T(8,128)S(1)}, f32[16,128]{1,0:T(8,128)S(1)}, u32[]{:S(2)}, u32[]{:S(2)}) collective-permute-start(f32[16,128]{1,0:T(8,128)S(1)} %add.3.refs_0_), channel_id=1, source_target_pairs={{0,96},{16,112},{32,0},{48,16},{64,32},{80,48},{96,64},{112,80},{1... | collective-permute-start | bytes 24584 | tf_op jit(solution)/shard_map/ppermute | solution.py:275
  12.0 0.0 collective-permute-done.4.received
  12.0 1.1 %shard_map.161.refs_4_ = bf16[32,32768]{1,0:T(8,128)(2,1)S(1)} custom-call(f32[16,32768]{1,0:T(8,128)S(1)} %collective-permute-done.4.received, f32[16,28672]{1,0:T(8,128)S(1)} %get-tuple-element.37.refs_0_.refs_2_, f32[16,28672]{1,0:T(8,128)S(1)} %get-tuple-element.38.refs_1_.refs_3_, f32[16,8192]{1,0:T(8,128)S(1)} %get-tuple-element.39.refs_2_.refs_4_), custom_call_target="tpu_custom_call" | custom-call | flops 10000000 | bytes 6291456 | tf_op jit(solution)/shard_map/pallas_call | solution.py:279
  13.1 0.0 collective-permute-done.1.refs_1_
  13.1 0.0 collective-permute-done.2.refs_2_
  13.1 0.5 collective-permute-done.3.refs_3_
  13.6 0.6 %shard_map.162 = f32[1088,128]{1,0:T(8,128)S(1)} custom-call(f32[16,128]{1,0:T(8,128)S(1)} %add.3.refs_0_, f32[16,128]{1,0:T(8,128)S(1)} %collective-permute-done.1.refs_1_, f32[16,128]{1,0:T(8,128)S(1)} %collective-permute-done.2.refs_2_, f32[16,128]{1,0:T(8,128)S(1)} %collective-permute-done.3.refs_3_, bf16[32,32768]{1,0:T(8,128)(2,1)S(1)} %shard_map.161.refs_4_), custom_call_target="tpu_custom_call" | custom-call | flops 10000000 | bytes 3145728 | tf_op jit(solution)/shard_map/pallas_call | solution.py:287
  14.2 17.5 %all_to_all.10 = f32[64,1,2176]{2,1,0:T(1,128)S(1)} all-to-all(f32[64,1,2176]{2,1,0:T(1,128)S(1)} %bitcast.5), channel_id=1, replica_groups={{74,73,72,75,70,69,68,71,66,65,64,67,78,77,76,79,42,41,40,43,38,37,36,3..., dimensions={0} | all-to-all | bytes 1114112 | tf_op jit(solution)/shard_map/all_to_all | solution.py:299
  31.7 0.3 shard_map.163
  32.0 14.9 %all_to_all.11 = f32[64,1,2048]{2,1,0:T(1,128)S(1)} all-to-all(f32[64,1,2048]{2,1,0:T(1,128)S(1)} %bitcast.8), channel_id=1, replica_groups={{74,73,72,75,70,69,68,71,66,65,64,67,78,77,76,79,42,41,40,43,38,37,36,3..., dimensions={0} | all-to-all | bytes 1048576 | tf_op jit(solution)/shard_map/all_to_all | solution.py:315
  46.9 4.0 %collective-permute-start.5 = (f32[1024,128]{1,0:T(8,128)S(1)}, f32[1024,128]{1,0:T(8,128)S(1)}, u32[]{:S(2)}, u32[]{:S(2)}) collective-permute-start(f32[1024,128]{1,0:T(8,128)S(1)} %bitcast.6), channel_id=1, source_target_pairs={{0,16},{16,0},{32,48},{48,32},{64,80},{80,64},{96,112},{112,96},{1... | collective-permute-start | bytes 1572872 | tf_op jit(solution)/shard_map/ppermute | solution.py:318
  50.9 1.9 %shard_map.164 = (f32[4,28672]{1,0:T(4,128)}, f32[4,28672]{1,0:T(4,128)}, f32[4,8192]{1,0:T(4,128)}, bf16[1,16,28672]{2,1,0:T(8,128)(2,1)}, bf16[1,16,28672]{2,1...) custom-call(f32[1024,128]{1,0:T(8,128)S(1)} %bitcast.7, ...), custom_call_target="tpu_custom_call" | custom-call | flops 10000000 | bytes 4194304 | tf_op jit(solution)/shard_map/pallas_call | solution.py:325
  52.8 0.0 collective-permute-done.5.refs_0_
  52.8 1.8 %shard_map.165 = (f32[4,28672]{1,0:T(4,128)}, f32[4,28672]{1,0:T(4,128)}, f32[4,8192]{1,0:T(4,128)}, bf16[1,16,28672]{2,1,0:T(8,128)(2,1)}, bf16[1,16,28672]{2,1,0:T(8,128)(2,1)}, /*index=5*/bf16[1,16,8192]{2,1,0:T(8,128)(2,1)}) custom-call(f32[1024,128]{1,0:T(8,128)S(1)} %collective-permute-done, ...), custom_call_target="tpu_custom_call", output_to_operand_aliasing={{0}: (5, {}), {1}: (6, {}), {2}: (7, {}), {3}: (8, {}), {4}... | custom-call | flops 10000000 | bytes 4194304 | tf_op jit(solution)/shard_map/pallas_call | solution.py:338
  (1 shorter events, 0.0 us)
Async XLA Ops:
  4.4 2.3 %collective-permute-start = (f32[16,128]{1,0:T(8,128)S(1)}, f32[16,128]{1,0:T(8,128)S(1)}, u32[]{:S(2)}, u32[]{:S(2)}) collective-permute-start(f32[16,128]{1,0:T(8,128)S(1)} %get-tuple-element.34), channel_id=1, source_target_pairs={{0,16},{16,0},{32,48},{48,32},{64,80},{80,64},{96,112},{112,96},{1... | collective-permute-start | bytes 24584 | tf_op jit(solution)/shard_map/ppermute | solution.py:271
  6.7 5.2 %collective-permute-start.4 = (f32[16,32768]{1,0:T(8,128)S(1)}, f32[16,32768]{1,0:T(8,128)S(1)}, u32[]{:S(2)}, u32[]{:S(2)}) collective-permute-start(f32[16,32768]{1,0:T(8,128)S(1)} %get-tuple-element.36), channel_id=1, source_target_pairs={{0,16},{16,0},{32,48},{48,32},{64,80},{80,64},{96,112},{112,96},{1... | collective-permute-start | bytes 6291464 | tf_op jit(solution)/shard_map/ppermute | solution.py:273
  7.1 6.0 %collective-permute-start.1 = (f32[16,128]{1,0:T(8,128)S(1)}, f32[16,128]{1,0:T(8,128)S(1)}, u32[]{:S(2)}, u32[]{:S(2)}) collective-permute-start(f32[16,128]{1,0:T(8,128)S(1)} %add.3.refs_0_), channel_id=1, source_target_pairs={{0,32},{16,48},{32,64},{48,80},{64,96},{80,112},{96,0},{112,16},{1... | collective-permute-start | bytes 24584 | tf_op jit(solution)/shard_map/ppermute | solution.py:275
  8.4 4.7 %collective-permute-start.2 = (f32[16,128]{1,0:T(8,128)S(1)}, f32[16,128]{1,0:T(8,128)S(1)}, u32[]{:S(2)}, u32[]{:S(2)}) collective-permute-start(f32[16,128]{1,0:T(8,128)S(1)} %add.3.refs_0_), channel_id=1, source_target_pairs={{0,64},{16,80},{32,96},{48,112},{64,0},{80,16},{96,32},{112,48},{1... | collective-permute-start | bytes 24584 | tf_op jit(solution)/shard_map/ppermute | solution.py:275
  10.8 2.8 %collective-permute-start.3 = (f32[16,128]{1,0:T(8,128)S(1)}, f32[16,128]{1,0:T(8,128)S(1)}, u32[]{:S(2)}, u32[]{:S(2)}) collective-permute-start(f32[16,128]{1,0:T(8,128)S(1)} %add.3.refs_0_), channel_id=1, source_target_pairs={{0,96},{16,112},{32,0},{48,16},{64,32},{80,48},{96,64},{112,80},{1... | collective-permute-start | bytes 24584 | tf_op jit(solution)/shard_map/ppermute | solution.py:275
  46.9 5.9 %collective-permute-start.5 = (f32[1024,128]{1,0:T(8,128)S(1)}, f32[1024,128]{1,0:T(8,128)S(1)}, u32[]{:S(2)}, u32[]{:S(2)}) collective-permute-start(f32[1024,128]{1,0:T(8,128)S(1)} %bitcast.6), channel_id=1, source_target_pairs={{0,16},{16,0},{32,48},{48,32},{64,80},{80,64},{96,112},{112,96},{1... | collective-permute-start | bytes 1572872 | tf_op jit(solution)/shard_map/ppermute | solution.py:318

commit v8 on v7

--- a/solution.py
+++ b/solution.py
@@ -183,7 +183,7 @@
         copies[16 * k : 16 * k + 16, :] = block
 
 
-OUT_PIECES = (4, 4, 1)
+OUT_PIECES = (1, 1, 1)
 
 
 def finish_kernel(own, *refs):

time: 54.8 us -> 54.7 us (level)
  no operation moved by 1% of the time
where the time goes in v8:
time: 54.7 us; the launch traced here: 54.5 us
  blocking collectives  32.4 us (59%)
  starting transfers between devices  10.8 us (20%)
  Pallas kernels  9.31 us (17%)
  waiting for transfers between devices  1.3 us (2%)
  between operations  0.71 us (1%)
    all_to_all x1, blocking collectives, per_device(): lax.all_to_all(chip_sum.reshape(CHIPS, 1, BLOCK_ROWS * LANES), both, 0, 0...  17.5 us
    all_to_all x1, blocking collectives, per_device(): lax.all_to_all(copies.reshape(CHIPS, 1, 16 * LANES), both, 0, 0, tiled=Tr...  14.9 us
    ppermute x3, starting transfers between devices, per_device(): lax.ppermute(chip_partial, 'dp', [(i, (i + 2 * k) % 8) for i in range(8)])  4.9 us
    ppermute x1, starting transfers between devices, per_device(): theirs = lax.ppermute(mine, 'dp', swap)  4.02 us
    pallas_call x1, Pallas kernels, per_device(): pl.pallas_call(merge_kernel, out_shape=[pltpu.VMEM((ROWS, c), F32) for c...  3.76 us
    pallas_call x1, Pallas kernels, per_device(): pl.pallas_call(functools.partial(finish_kernel, True), out_shape=next_sha...  1.82 us
    pallas_call x1, Pallas kernels, per_device(): pl.pallas_call(functools.partial(finish_kernel, False), out_shape=next_sh...  1.78 us
    ppermute x1, starting transfers between devices, per_device(): chip_partial = partial + lax.ppermute(partial, 'dp', swap)  1.5 us
  transfers between devices with their start and end apart: 6, of which 2 were waited for; matrix products, arithmetic and copies ran while one was open for 0% of the time, Pallas kernels for 5%

profile of v8, /device:TPU:1, one launch (start us, length us, event | category | flops | bytes accessed | tf_op | source)
XLA Modules:
  0.0 54.5 jit_solution(3837508686583837720)
XLA Ops:
  0.6 3.8 %shard_map.160 = (f32[16,28672]{1,0:T(8,128)S(1)}, f32[16,28672]{1,0:T(8,128)S(1)}, f32[16,8192]{1,0:T(8,128)S(1)}, f32[16,32768]{1,0:T(8,128)S(1)}, f32[16,128]{1,0:T(8,128)S(1)}) custom-call(f32[1,16,28672]{2,1,0:T(8,128)} %refs_0_.1, f32[1,16,28672]{2,1,0:T(8,128)} %refs_1_.1, f32[1,16,8192]{2,1,0:T(8,128)} %refs_2_.1, bf16[1,16,28672]{2,1,0:T(8,128)(2,1)} %refs_3_.1, ...), custom_call_target="tpu_custom_call" | custom-call | flops 10000000 | bytes 7340032 | tf_op jit(solution)/shard_map/pallas_call | solution.py:257
  4.4 1.5 %collective-permute-start = (f32[16,128]{1,0:T(8,128)S(1)}, f32[16,128]{1,0:T(8,128)S(1)}, u32[]{:S(2)}, u32[]{:S(2)}) collective-permute-start(f32[16,128]{1,0:T(8,128)S(1)} %get-tuple-element.34), channel_id=1, source_target_pairs={{0,16},{16,0},{32,48},{48,32},{64,80},{80,64},{96,112},{112,96},{1... | collective-permute-start | bytes 24584 | tf_op jit(solution)/shard_map/ppermute | solution.py:271
  5.9 0.8 %collective-permute-done = f32[16,128]{1,0:T(8,128)S(1)} collective-permute-done((f32[16,128]{1,0:T(8,128)S(1)}, f32[16,128]{1,0:T(8,128)S(1)}, u32[]{:S(2)}, u32[]{:S(2)}) %collective-permute-start) | collective-permute-done | bytes 8224 | tf_op jit(solution)/shard_map/ppermute | solution.py:271
  6.7 0.3 collective-permute-start.4
  7.1 1.3 %collective-permute-start.1 = (f32[16,128]{1,0:T(8,128)S(1)}, f32[16,128]{1,0:T(8,128)S(1)}, u32[]{:S(2)}, u32[]{:S(2)}) collective-permute-start(f32[16,128]{1,0:T(8,128)S(1)} %add.3.refs_0_), channel_id=1, source_target_pairs={{0,32},{16,48},{32,64},{48,80},{64,96},{80,112},{96,0},{112,16},{1... | collective-permute-start | bytes 24584 | tf_op jit(solution)/shard_map/ppermute | solution.py:275
  8.4 2.5 %collective-permute-start.2 = (f32[16,128]{1,0:T(8,128)S(1)}, f32[16,128]{1,0:T(8,128)S(1)}, u32[]{:S(2)}, u32[]{:S(2)}) collective-permute-start(f32[16,128]{1,0:T(8,128)S(1)} %add.3.refs_0_), channel_id=1, source_target_pairs={{0,64},{16,80},{32,96},{48,112},{64,0},{80,16},{96,32},{112,48},{1... | collective-permute-start | bytes 24584 | tf_op jit(solution)/shard_map/ppermute | solution.py:275
  10.8 1.2 %collective-permute-start.3 = (f32[16,128]{1,0:T(8,128)S(1)}, f32[16,128]{1,0:T(8,128)S(1)}, u32[]{:S(2)}, u32[]{:S(2)}) collective-permute-start(f32[16,128]{1,0:T(8,128)S(1)} %add.3.refs_0_), channel_id=1, source_target_pairs={{0,96},{16,112},{32,0},{48,16},{64,32},{80,48},{96,64},{112,80},{1... | collective-permute-start | bytes 24584 | tf_op jit(solution)/shard_map/ppermute | solution.py:275
  12.0 0.0 collective-permute-done.4.received
  12.0 1.1 %shard_map.161.refs_4_ = bf16[32,32768]{1,0:T(8,128)(2,1)S(1)} custom-call(f32[16,32768]{1,0:T(8,128)S(1)} %collective-permute-done.4.received, f32[16,28672]{1,0:T(8,128)S(1)} %get-tuple-element.37.refs_0_.refs_2_, f32[16,28672]{1,0:T(8,128)S(1)} %get-tuple-element.38.refs_1_.refs_3_, f32[16,8192]{1,0:T(8,128)S(1)} %get-tuple-element.39.refs_2_.refs_4_), custom_call_target="tpu_custom_call" | custom-call | flops 10000000 | bytes 6291456 | tf_op jit(solution)/shard_map/pallas_call | solution.py:279
  13.1 0.0 collective-permute-done.1.refs_1_
  13.1 0.0 collective-permute-done.2.refs_2_
  13.1 0.5 collective-permute-done.3.refs_3_
  13.6 0.6 %shard_map.162 = f32[1088,128]{1,0:T(8,128)S(1)} custom-call(f32[16,128]{1,0:T(8,128)S(1)} %add.3.refs_0_, f32[16,128]{1,0:T(8,128)S(1)} %collective-permute-done.1.refs_1_, f32[16,128]{1,0:T(8,128)S(1)} %collective-permute-done.2.refs_2_, f32[16,128]{1,0:T(8,128)S(1)} %collective-permute-done.3.refs_3_, bf16[32,32768]{1,0:T(8,128)(2,1)S(1)} %shard_map.161.refs_4_), custom_call_target="tpu_custom_call" | custom-call | flops 10000000 | bytes 3145728 | tf_op jit(solution)/shard_map/pallas_call | solution.py:287
  14.2 17.5 %all_to_all.10 = f32[64,1,2176]{2,1,0:T(1,128)S(1)} all-to-all(f32[64,1,2176]{2,1,0:T(1,128)S(1)} %bitcast.5), channel_id=1, replica_groups={{74,73,72,75,70,69,68,71,66,65,64,67,78,77,76,79,42,41,40,43,38,37,36,3..., dimensions={0} | all-to-all | bytes 1114112 | tf_op jit(solution)/shard_map/all_to_all | solution.py:299
  31.7 0.3 shard_map.163
  32.0 14.9 %all_to_all.11 = f32[64,1,2048]{2,1,0:T(1,128)S(1)} all-to-all(f32[64,1,2048]{2,1,0:T(1,128)S(1)} %bitcast.8), channel_id=1, replica_groups={{74,73,72,75,70,69,68,71,66,65,64,67,78,77,76,79,42,41,40,43,38,37,36,3..., dimensions={0} | all-to-all | bytes 1048576 | tf_op jit(solution)/shard_map/all_to_all | solution.py:315
  46.9 4.0 %collective-permute-start.5 = (f32[1024,128]{1,0:T(8,128)S(1)}, f32[1024,128]{1,0:T(8,128)S(1)}, u32[]{:S(2)}, u32[]{:S(2)}) collective-permute-start(f32[1024,128]{1,0:T(8,128)S(1)} %bitcast.6), channel_id=1, source_target_pairs={{0,16},{16,0},{32,48},{48,32},{64,80},{80,64},{96,112},{112,96},{1... | collective-permute-start | bytes 1572872 | tf_op jit(solution)/shard_map/ppermute | solution.py:318
  50.9 1.8 %shard_map.164 = (f32[4,28672]{1,0:T(4,128)}, f32[4,28672]{1,0:T(4,128)}, f32[4,8192]{1,0:T(4,128)}, bf16[1,16,28672]{2,1,0:T(8,128)(2,1)}, bf16[1,16,28672]{2,1...) custom-call(f32[1024,128]{1,0:T(8,128)S(1)} %bitcast.7, ...), custom_call_target="tpu_custom_call" | custom-call | flops 10000000 | bytes 4194304 | tf_op jit(solution)/shard_map/pallas_call | solution.py:325
  52.7 0.0 collective-permute-done.5.refs_0_
  52.7 1.8 %shard_map.165 = (f32[4,28672]{1,0:T(4,128)}, f32[4,28672]{1,0:T(4,128)}, f32[4,8192]{1,0:T(4,128)}, bf16[1,16,28672]{2,1,0:T(8,128)(2,1)}, bf16[1,16,28672]{2,1,0:T(8,128)(2,1)}, /*index=5*/bf16[1,16,8192]{2,1,0:T(8,128)(2,1)}) custom-call(f32[1024,128]{1,0:T(8,128)S(1)} %collective-permute-done, ...), custom_call_target="tpu_custom_call", output_to_operand_aliasing={{0}: (5, {}), {1}: (6, {}), {2}: (7, {}), {3}: (8, {}), {4}... | custom-call | flops 10000000 | bytes 4194304 | tf_op jit(solution)/shard_map/pallas_call | solution.py:338
  (1 shorter events, 0.0 us)
Async XLA Ops:
  4.4 2.3 %collective-permute-start = (f32[16,128]{1,0:T(8,128)S(1)}, f32[16,128]{1,0:T(8,128)S(1)}, u32[]{:S(2)}, u32[]{:S(2)}) collective-permute-start(f32[16,128]{1,0:T(8,128)S(1)} %get-tuple-element.34), channel_id=1, source_target_pairs={{0,16},{16,0},{32,48},{48,32},{64,80},{80,64},{96,112},{112,96},{1... | collective-permute-start | bytes 24584 | tf_op jit(solution)/shard_map/ppermute | solution.py:271
  6.7 5.2 %collective-permute-start.4 = (f32[16,32768]{1,0:T(8,128)S(1)}, f32[16,32768]{1,0:T(8,128)S(1)}, u32[]{:S(2)}, u32[]{:S(2)}) collective-permute-start(f32[16,32768]{1,0:T(8,128)S(1)} %get-tuple-element.36), channel_id=1, source_target_pairs={{0,16},{16,0},{32,48},{48,32},{64,80},{80,64},{96,112},{112,96},{1... | collective-permute-start | bytes 6291464 | tf_op jit(solution)/shard_map/ppermute | solution.py:273
  7.1 6.0 %collective-permute-start.1 = (f32[16,128]{1,0:T(8,128)S(1)}, f32[16,128]{1,0:T(8,128)S(1)}, u32[]{:S(2)}, u32[]{:S(2)}) collective-permute-start(f32[16,128]{1,0:T(8,128)S(1)} %add.3.refs_0_), channel_id=1, source_target_pairs={{0,32},{16,48},{32,64},{48,80},{64,96},{80,112},{96,0},{112,16},{1... | collective-permute-start | bytes 24584 | tf_op jit(solution)/shard_map/ppermute | solution.py:275
  8.4 4.7 %collective-permute-start.2 = (f32[16,128]{1,0:T(8,128)S(1)}, f32[16,128]{1,0:T(8,128)S(1)}, u32[]{:S(2)}, u32[]{:S(2)}) collective-permute-start(f32[16,128]{1,0:T(8,128)S(1)} %add.3.refs_0_), channel_id=1, source_target_pairs={{0,64},{16,80},{32,96},{48,112},{64,0},{80,16},{96,32},{112,48},{1... | collective-permute-start | bytes 24584 | tf_op jit(solution)/shard_map/ppermute | solution.py:275
  10.8 2.8 %collective-permute-start.3 = (f32[16,128]{1,0:T(8,128)S(1)}, f32[16,128]{1,0:T(8,128)S(1)}, u32[]{:S(2)}, u32[]{:S(2)}) collective-permute-start(f32[16,128]{1,0:T(8,128)S(1)} %add.3.refs_0_), channel_id=1, source_target_pairs={{0,96},{16,112},{32,0},{48,16},{64,32},{80,48},{96,64},{112,80},{1... | collective-permute-start | bytes 24584 | tf_op jit(solution)/shard_map/ppermute | solution.py:275
  46.9 5.9 %collective-permute-start.5 = (f32[1024,128]{1,0:T(8,128)S(1)}, f32[1024,128]{1,0:T(8,128)S(1)}, u32[]{:S(2)}, u32[]{:S(2)}) collective-permute-start(f32[1024,128]{1,0:T(8,128)S(1)} %bitcast.6), channel_id=1, source_target_pairs={{0,16},{16,0},{32,48},{48,32},{64,80},{80,64},{96,112},{112,96},{1... | collective-permute-start | bytes 1572872 | tf_op jit(solution)/shard_map/ppermute | solution.py:318

commit v9 on v8

--- a/solution.py
+++ b/solution.py
@@ -135,7 +135,7 @@
     for k in range(CHIPS):
         total[k % 4] = total[k % 4] + blocks[k * BLOCK_ROWS : k * BLOCK_ROWS + 16, :]
         grams[k % 4] = grams[k % 4] + blocks[k * BLOCK_ROWS + 16 : k * BLOCK_ROWS + 17, :]
-    scratch[...] = (total[0] + total[1]) + (total[2] + total[3])
+    scratch[0:16, :] = (total[0] + total[1]) + (total[2] + total[3])
     gram = ((grams[0] + grams[1]) + (grams[2] + grams[3])) * 0.25
 
     def entry(i, j):
@@ -178,7 +178,7 @@
         nexts.append(current / value)
     for i in range(RANK):
         scratch[pl.ds(i, 4, stride=4), :] = nexts[i]
-    block = scratch[...]
+    block = scratch[0:16, :]
     for k in range(CHIPS):
         copies[16 * k : 16 * k + 16, :] = block
 
@@ -216,17 +216,20 @@
         for piece in range(OUT_PIECES[m]):
 
             def step(j, carry, m=m, piece=piece, columns=columns, size=size):
-                local = pl.multiple_of(piece * size + j * LANES, LANES)
-                value = merged[m][:, pl.ds(pl.multiple_of(half * (COLS[m] // 2) + local, LANES), LANES)]
-                row = FIRST_BLOCK[m] * 16 + piece * (size // LANES) * RANK + j * RANK
-                nbuf[m][:, pl.ds(local, LANES)] = rows[pl.ds(row, RANK), :]
-                approx = columns[0] * rows[pl.ds(row, 1), :]
-                for i in range(1, RANK):
-                    approx = approx + columns[i] * rows[pl.ds(row + i, 1), :]
-                ebuf[m][:, pl.ds(local, LANES)] = (value - approx).astype(BF16)
+                row = FIRST_BLOCK[m] * 16 + piece * (size // LANES) * RANK + j * 8
+                both = rows[pl.ds(pl.multiple_of(row, 8), 8), :]
+                for b in range(2):
+                    local = pl.multiple_of(piece * size + (2 * j + b) * LANES, LANES)
+                    value = merged[m][:, pl.ds(pl.multiple_of(half * (COLS[m] // 2) + local, LANES), LANES)]
+                    four = both[b * RANK : (b + 1) * RANK]
+                    nbuf[m][:, pl.ds(local, LANES)] = four
+                    approx = columns[0] * four[0:1]
+                    for i in range(1, RANK):
+                        approx = approx + columns[i] * four[i : i + 1]
+                    ebuf[m][:, pl.ds(local, LANES)] = (value - approx).astype(BF16)
                 return carry
 
-            lax.fori_loop(0, size // LANES, step, 0, unroll=14 if m < 2 else 16)
+            lax.fori_loop(0, size // LANES // 2, step, 0, unroll=8)
             here = pl.ds(piece * size, size)
             there = pl.ds(pl.multiple_of(half * (COLS[m] // 2) + piece * size, LANES), size)
             for copy in (
@@ -308,7 +311,7 @@
         ],
         in_specs=[VMEM] * 5,
         out_specs=[VMEM] * 2,
-        scratch_shapes=[pltpu.VMEM((16, LANES), F32)],
+        scratch_shapes=[pltpu.VMEM((24, LANES), F32)],
         compiler_params=PARAMS,
         cost_estimate=cost(10**6, 2**20),
     )(blocks, *gathered)

time: 54.7 us -> 54.7 us (level)
  no operation moved by 1% of the time
where the time goes in v9:
time: 54.7 us; the launch traced here: 54.5 us
  blocking collectives  32.4 us (59%)
  starting transfers between devices  10.8 us (20%)
  Pallas kernels  9.34 us (17%)
  waiting for transfers between devices  1.3 us (2%)
  between operations  0.71 us (1%)
    all_to_all x1, blocking collectives, per_device(): lax.all_to_all(chip_sum.reshape(CHIPS, 1, BLOCK_ROWS * LANES), both, 0, 0...  17.5 us
    all_to_all x1, blocking collectives, per_device(): lax.all_to_all(copies.reshape(CHIPS, 1, 16 * LANES), both, 0, 0, tiled=Tr...  14.9 us
    ppermute x3, starting transfers between devices, per_device(): lax.ppermute(chip_partial, 'dp', [(i, (i + 2 * k) % 8) for i in range(8)])  4.9 us
    ppermute x1, starting transfers between devices, per_device(): theirs = lax.ppermute(mine, 'dp', swap)  4.02 us
    pallas_call x1, Pallas kernels, per_device(): pl.pallas_call(merge_kernel, out_shape=[pltpu.VMEM((ROWS, c), F32) for c...  3.76 us
    pallas_call x1, Pallas kernels, per_device(): pl.pallas_call(functools.partial(finish_kernel, True), out_shape=next_sha...  1.83 us
    pallas_call x1, Pallas kernels, per_device(): pl.pallas_call(functools.partial(finish_kernel, False), out_shape=next_sh...  1.8 us
    ppermute x1, starting transfers between devices, per_device(): chip_partial = partial + lax.ppermute(partial, 'dp', swap)  1.5 us
  transfers between devices with their start and end apart: 6, of which 2 were waited for; matrix products, arithmetic and copies ran while one was open for 0% of the time, Pallas kernels for 5%

profile of v9, /device:TPU:1, one launch (start us, length us, event | category | flops | bytes accessed | tf_op | source)
XLA Modules:
  0.0 54.5 jit_solution(14874363305538322349)
XLA Ops:
  0.6 3.8 %shard_map.160 = (f32[16,28672]{1,0:T(8,128)S(1)}, f32[16,28672]{1,0:T(8,128)S(1)}, f32[16,8192]{1,0:T(8,128)S(1)}, f32[16,32768]{1,0:T(8,128)S(1)}, f32[16,128]{1,0:T(8,128)S(1)}) custom-call(f32[1,16,28672]{2,1,0:T(8,128)} %refs_0_.1, f32[1,16,28672]{2,1,0:T(8,128)} %refs_1_.1, f32[1,16,8192]{2,1,0:T(8,128)} %refs_2_.1, bf16[1,16,28672]{2,1,0:T(8,128)(2,1)} %refs_3_.1, ...), custom_call_target="tpu_custom_call" | custom-call | flops 10000000 | bytes 7340032 | tf_op jit(solution)/shard_map/pallas_call | solution.py:260
  4.4 1.5 %collective-permute-start = (f32[16,128]{1,0:T(8,128)S(1)}, f32[16,128]{1,0:T(8,128)S(1)}, u32[]{:S(2)}, u32[]{:S(2)}) collective-permute-start(f32[16,128]{1,0:T(8,128)S(1)} %get-tuple-element.34), channel_id=1, source_target_pairs={{0,16},{16,0},{32,48},{48,32},{64,80},{80,64},{96,112},{112,96},{1... | collective-permute-start | bytes 24584 | tf_op jit(solution)/shard_map/ppermute | solution.py:274
  5.9 0.8 %collective-permute-done = f32[16,128]{1,0:T(8,128)S(1)} collective-permute-done((f32[16,128]{1,0:T(8,128)S(1)}, f32[16,128]{1,0:T(8,128)S(1)}, u32[]{:S(2)}, u32[]{:S(2)}) %collective-permute-start) | collective-permute-done | bytes 8224 | tf_op jit(solution)/shard_map/ppermute | solution.py:274
  6.7 0.3 collective-permute-start.4
  7.1 1.3 %collective-permute-start.1 = (f32[16,128]{1,0:T(8,128)S(1)}, f32[16,128]{1,0:T(8,128)S(1)}, u32[]{:S(2)}, u32[]{:S(2)}) collective-permute-start(f32[16,128]{1,0:T(8,128)S(1)} %add.3.refs_0_), channel_id=1, source_target_pairs={{0,32},{16,48},{32,64},{48,80},{64,96},{80,112},{96,0},{112,16},{1... | collective-permute-start | bytes 24584 | tf_op jit(solution)/shard_map/ppermute | solution.py:278
  8.4 2.5 %collective-permute-start.2 = (f32[16,128]{1,0:T(8,128)S(1)}, f32[16,128]{1,0:T(8,128)S(1)}, u32[]{:S(2)}, u32[]{:S(2)}) collective-permute-start(f32[16,128]{1,0:T(8,128)S(1)} %add.3.refs_0_), channel_id=1, source_target_pairs={{0,64},{16,80},{32,96},{48,112},{64,0},{80,16},{96,32},{112,48},{1... | collective-permute-start | bytes 24584 | tf_op jit(solution)/shard_map/ppermute | solution.py:278
  10.8 1.2 %collective-permute-start.3 = (f32[16,128]{1,0:T(8,128)S(1)}, f32[16,128]{1,0:T(8,128)S(1)}, u32[]{:S(2)}, u32[]{:S(2)}) collective-permute-start(f32[16,128]{1,0:T(8,128)S(1)} %add.3.refs_0_), channel_id=1, source_target_pairs={{0,96},{16,112},{32,0},{48,16},{64,32},{80,48},{96,64},{112,80},{1... | collective-permute-start | bytes 24584 | tf_op jit(solution)/shard_map/ppermute | solution.py:278
  12.0 0.0 collective-permute-done.4.received
  12.0 1.1 %shard_map.161.refs_4_ = bf16[32,32768]{1,0:T(8,128)(2,1)S(1)} custom-call(f32[16,32768]{1,0:T(8,128)S(1)} %collective-permute-done.4.received, f32[16,28672]{1,0:T(8,128)S(1)} %get-tuple-element.37.refs_0_.refs_2_, f32[16,28672]{1,0:T(8,128)S(1)} %get-tuple-element.38.refs_1_.refs_3_, f32[16,8192]{1,0:T(8,128)S(1)} %get-tuple-element.39.refs_2_.refs_4_), custom_call_target="tpu_custom_call" | custom-call | flops 10000000 | bytes 6291456 | tf_op jit(solution)/shard_map/pallas_call | solution.py:282
  13.1 0.0 collective-permute-done.1.refs_1_
  13.1 0.0 collective-permute-done.2.refs_2_
  13.1 0.5 collective-permute-done.3.refs_3_
  13.6 0.6 %shard_map.162 = f32[1088,128]{1,0:T(8,128)S(1)} custom-call(f32[16,128]{1,0:T(8,128)S(1)} %add.3.refs_0_, f32[16,128]{1,0:T(8,128)S(1)} %collective-permute-done.1.refs_1_, f32[16,128]{1,0:T(8,128)S(1)} %collective-permute-done.2.refs_2_, f32[16,128]{1,0:T(8,128)S(1)} %collective-permute-done.3.refs_3_, bf16[32,32768]{1,0:T(8,128)(2,1)S(1)} %shard_map.161.refs_4_), custom_call_target="tpu_custom_call" | custom-call | flops 10000000 | bytes 3145728 | tf_op jit(solution)/shard_map/pallas_call | solution.py:290
  14.2 17.5 %all_to_all.10 = f32[64,1,2176]{2,1,0:T(1,128)S(1)} all-to-all(f32[64,1,2176]{2,1,0:T(1,128)S(1)} %bitcast.5), channel_id=1, replica_groups={{74,73,72,75,70,69,68,71,66,65,64,67,78,77,76,79,42,41,40,43,38,37,36,3..., dimensions={0} | all-to-all | bytes 1114112 | tf_op jit(solution)/shard_map/all_to_all | solution.py:302
  31.7 0.3 shard_map.163
  32.0 14.9 %all_to_all.11 = f32[64,1,2048]{2,1,0:T(1,128)S(1)} all-to-all(f32[64,1,2048]{2,1,0:T(1,128)S(1)} %bitcast.8), channel_id=1, replica_groups={{74,73,72,75,70,69,68,71,66,65,64,67,78,77,76,79,42,41,40,43,38,37,36,3..., dimensions={0} | all-to-all | bytes 1048576 | tf_op jit(solution)/shard_map/all_to_all | solution.py:318
  46.9 4.0 %collective-permute-start.5 = (f32[1024,128]{1,0:T(8,128)S(1)}, f32[1024,128]{1,0:T(8,128)S(1)}, u32[]{:S(2)}, u32[]{:S(2)}) collective-permute-start(f32[1024,128]{1,0:T(8,128)S(1)} %bitcast.6), channel_id=1, source_target_pairs={{0,16},{16,0},{32,48},{48,32},{64,80},{80,64},{96,112},{112,96},{1... | collective-permute-start | bytes 1572872 | tf_op jit(solution)/shard_map/ppermute | solution.py:321
  50.9 1.8 %shard_map.164 = (f32[4,28672]{1,0:T(4,128)}, f32[4,28672]{1,0:T(4,128)}, f32[4,8192]{1,0:T(4,128)}, bf16[1,16,28672]{2,1,0:T(8,128)(2,1)}, bf16[1,16,28672]{2,1...) custom-call(f32[1024,128]{1,0:T(8,128)S(1)} %bitcast.7, ...), custom_call_target="tpu_custom_call" | custom-call | flops 10000000 | bytes 4194304 | tf_op jit(solution)/shard_map/pallas_call | solution.py:328
  52.7 0.0 collective-permute-done.5.refs_0_
  52.7 1.8 %shard_map.165 = (f32[4,28672]{1,0:T(4,128)}, f32[4,28672]{1,0:T(4,128)}, f32[4,8192]{1,0:T(4,128)}, bf16[1,16,28672]{2,1,0:T(8,128)(2,1)}, bf16[1,16,28672]{2,1,0:T(8,128)(2,1)}, /*index=5*/bf16[1,16,8192]{2,1,0:T(8,128)(2,1)}) custom-call(f32[1024,128]{1,0:T(8,128)S(1)} %collective-permute-done, ...), custom_call_target="tpu_custom_call", output_to_operand_aliasing={{0}: (5, {}), {1}: (6, {}), {2}: (7, {}), {3}: (8, {}), {4}... | custom-call | flops 10000000 | bytes 4194304 | tf_op jit(solution)/shard_map/pallas_call | solution.py:341
  (1 shorter events, 0.0 us)
Async XLA Ops:
  4.4 2.3 %collective-permute-start = (f32[16,128]{1,0:T(8,128)S(1)}, f32[16,128]{1,0:T(8,128)S(1)}, u32[]{:S(2)}, u32[]{:S(2)}) collective-permute-start(f32[16,128]{1,0:T(8,128)S(1)} %get-tuple-element.34), channel_id=1, source_target_pairs={{0,16},{16,0},{32,48},{48,32},{64,80},{80,64},{96,112},{112,96},{1... | collective-permute-start | bytes 24584 | tf_op jit(solution)/shard_map/ppermute | solution.py:274
  6.7 5.2 %collective-permute-start.4 = (f32[16,32768]{1,0:T(8,128)S(1)}, f32[16,32768]{1,0:T(8,128)S(1)}, u32[]{:S(2)}, u32[]{:S(2)}) collective-permute-start(f32[16,32768]{1,0:T(8,128)S(1)} %get-tuple-element.36), channel_id=1, source_target_pairs={{0,16},{16,0},{32,48},{48,32},{64,80},{80,64},{96,112},{112,96},{1... | collective-permute-start | bytes 6291464 | tf_op jit(solution)/shard_map/ppermute | solution.py:276
  7.1 6.0 %collective-permute-start.1 = (f32[16,128]{1,0:T(8,128)S(1)}, f32[16,128]{1,0:T(8,128)S(1)}, u32[]{:S(2)}, u32[]{:S(2)}) collective-permute-start(f32[16,128]{1,0:T(8,128)S(1)} %add.3.refs_0_), channel_id=1, source_target_pairs={{0,32},{16,48},{32,64},{48,80},{64,96},{80,112},{96,0},{112,16},{1... | collective-permute-start | bytes 24584 | tf_op jit(solution)/shard_map/ppermute | solution.py:278
  8.4 4.7 %collective-permute-start.2 = (f32[16,128]{1,0:T(8,128)S(1)}, f32[16,128]{1,0:T(8,128)S(1)}, u32[]{:S(2)}, u32[]{:S(2)}) collective-permute-start(f32[16,128]{1,0:T(8,128)S(1)} %add.3.refs_0_), channel_id=1, source_target_pairs={{0,64},{16,80},{32,96},{48,112},{64,0},{80,16},{96,32},{112,48},{1... | collective-permute-start | bytes 24584 | tf_op jit(solution)/shard_map/ppermute | solution.py:278
  10.8 2.8 %collective-permute-start.3 = (f32[16,128]{1,0:T(8,128)S(1)}, f32[16,128]{1,0:T(8,128)S(1)}, u32[]{:S(2)}, u32[]{:S(2)}) collective-permute-start(f32[16,128]{1,0:T(8,128)S(1)} %add.3.refs_0_), channel_id=1, source_target_pairs={{0,96},{16,112},{32,0},{48,16},{64,32},{80,48},{96,64},{112,80},{1... | collective-permute-start | bytes 24584 | tf_op jit(solution)/shard_map/ppermute | solution.py:278
  46.9 5.9 %collective-permute-start.5 = (f32[1024,128]{1,0:T(8,128)S(1)}, f32[1024,128]{1,0:T(8,128)S(1)}, u32[]{:S(2)}, u32[]{:S(2)}) collective-permute-start(f32[1024,128]{1,0:T(8,128)S(1)} %bitcast.6), channel_id=1, source_target_pairs={{0,16},{16,0},{32,48},{48,32},{64,80},{80,64},{96,112},{112,96},{1... | collective-permute-start | bytes 1572872 | tf_op jit(solution)/shard_map/ppermute | solution.py:321
